TPU v7x, 1024 devices: a whole 8x8x8 slice. The times are simulated.
1024 devices in a mesh: wide: 64 (over x, z), cross: 16 (over y, core).
Axes of the slice: x: 8, y: 8, z: 8, core: 2. Of those that a mesh axis runs over, the one named last changes fastest.
Arguments:
- populations: float32 [19, 1024, 8192], P(None, 'wide', 'cross'), may hold values from 0.019 to 0.44, as said below
- relaxation: float32 [1024, 8192], P('wide', 'cross'), may hold values from 0.5 to 1.5
- link_flags: int32 [2, 1024, 8192], P(None, 'wide', 'cross'), may hold values from 0 to 1023, as said below
- migrations: int32 [64, 16, 2], P('wide', 'cross'), may hold values from -1 to 1, as said below
Outputs:
- final_state: float32 [19, 1024, 8192], P(None, 'wide', 'cross')
- guest_block: float32 [19, 1024, 4096], P(None, 'wide', 'cross')
Inputs may be any that keep to these rules, and one draw needn't show every extreme that they name: `populations`: populations lie within 0.7 to 1.3 times their lattice weight. `link_flags`: bits agree with the solid cells: a population's bit is set exactly where the cell it pulls from is solid or outside the lattice. `migrations`: entry 0 is a block index below 2, entry 1 is -1, 0 or 1; no device sends past the ends of the wide axis, and no device receives more than one block.
All inputs are finite; a program needn't handle non-finite values.
Results may differ from a plain program's by a relative error of at most 0.00012.
Values sent between devices are 32-bit elements; how exact they have to be, the bound alone decides.
A program may use at most 64 MiB of HBM per device.

v0:
```python
import jax
import jax.numpy as jnp
from jax import lax
from jax.sharding import PartitionSpec as P

BLOCK = 16
BZ = 2
STEPS = 3


VELOCITY = (
    (0, 0, 0),
    (1, 0, 0),
    (-1, 0, 0),
    (0, 1, 0),
    (0, -1, 0),
    (0, 0, 1),
    (0, 0, -1),
    (1, 1, 0),
    (-1, -1, 0),
    (1, -1, 0),
    (-1, 1, 0),
    (1, 0, 1),
    (-1, 0, -1),
    (1, 0, -1),
    (-1, 0, 1),
    (0, 1, 1),
    (0, -1, -1),
    (0, 1, -1),
    (0, -1, 1),
)
OPPOSITE = (0, 2, 1, 4, 3, 6, 5, 8, 7, 10, 9, 12, 11, 14, 13, 16, 15, 18, 17)
LATTICE_WEIGHT = (1.0 / 3.0,) + (1.0 / 18.0,) * 6 + (1.0 / 36.0,) * 12


def extended(block, sides, width):
    for axis, dim in sides:
        count = lax.axis_size(axis)
        forward = [(i, i + 1) for i in range(count - 1)]
        backward = [(target, source) for source, target in forward]
        low = lax.ppermute(
            lax.slice_in_dim(block, block.shape[dim] - width, None, axis=dim), axis, forward
        )
        high = lax.ppermute(lax.slice_in_dim(block, 0, width, axis=dim), axis, backward)
        block = jnp.concatenate([low, block, high], axis=dim)
    return block


def from_behind(block, axis, distance):
    devices = range(lax.axis_size(axis))
    route = [(i - distance, i) for i in devices if i - distance in devices]
    return lax.ppermute(block, axis, route)


def collide(state, relaxation, fluid):
    density = jnp.sum(state, axis=0)
    divisor = jnp.where(fluid, density, 1.0)
    moments = []
    for axis_number in range(3):
        total = jnp.zeros_like(density)
        for number in range(19):
            factor = VELOCITY[number][axis_number]
            if factor != 0:
                total = total + factor * state[number]
        moments.append(total / divisor)
    square = moments[0] * moments[0] + moments[1] * moments[1] + moments[2] * moments[2]
    result = []
    for number in range(19):
        project = jnp.zeros_like(density)
        for axis_number in range(3):
            factor = VELOCITY[number][axis_number]
            if factor != 0:
                project = project + factor * moments[axis_number]
        balance = (
            LATTICE_WEIGHT[number]
            * density
            * (1.0 + 3.0 * project + 4.5 * project * project - 1.5 * square)
        )
        result.append(jnp.where(fluid, state[number] + relaxation * (balance - state[number]), 0.0))
    return jnp.stack(result)


def stream(padded, post, flags_low, flags_high, fluid, width, span, depth):
    place = lax.broadcasted_iota(jnp.int32, fluid.shape, 1) % depth
    result = []
    for number in range(19):
        step_x, step_y, step_z = VELOCITY[number]
        begin = (1 - step_y) * depth
        pulled = padded[number, 1 - step_x : 1 - step_x + width, begin : begin + span]
        if step_z == 1:
            pulled = jnp.concatenate([jnp.zeros_like(pulled[:, :1]), pulled[:, :-1]], axis=-1)
            pulled = jnp.where(place == 0, 0.0, pulled)
        elif step_z == -1:
            pulled = jnp.concatenate([pulled[:, 1:], jnp.zeros_like(pulled[:, :1])], axis=-1)
            pulled = jnp.where(place == depth - 1, 0.0, pulled)
        if number < 10:
            blocked = jnp.bitwise_and(jnp.right_shift(flags_low, number), 1) == 1
        else:
            blocked = jnp.bitwise_and(jnp.right_shift(flags_high, number - 10), 1) == 1
        value = jnp.where(blocked, post[OPPOSITE[number]], pulled)
        result.append(jnp.where(fluid, value, 0.0))
    return jnp.stack(result)


def local(populations, relaxation, link_flags, migrations):
    rows = populations.shape[1]
    depth = BLOCK * BZ
    span = populations.shape[2]
    height = span // depth
    state = populations
    flags_low = link_flags[0]
    flags_high = link_flags[1]
    fluid = jnp.bitwise_and(flags_low, 1) == 0
    for step_number in range(STEPS):
        post = collide(state, relaxation, fluid)
        framed = extended(post.reshape(19, rows, height, depth), (("wide", 1), ("cross", 2)), 1)
        padded = framed.reshape(19, rows + 2, (height + 2) * depth)
        state = stream(padded, post, flags_low, flags_high, fluid, rows, span, depth)
    chosen_index = migrations[0, 0, 0]
    heading = migrations[0, 0, 1]
    cubic = state.reshape(19, rows, height, depth)
    piece = lax.dynamic_slice_in_dim(cubic, chosen_index * BLOCK, BLOCK, 3).reshape(
        19, rows, height * BLOCK
    )
    eastward = jnp.where(heading == 1, piece, 0.0)
    westward = jnp.where(heading == -1, piece, 0.0)
    arrived = from_behind(eastward, "wide", 1) + from_behind(westward, "wide", -1)
    layer = lax.broadcasted_iota(jnp.int32, (span,), 0) % depth // BLOCK
    departed = (layer == chosen_index) & (heading != 0)
    final_state = jnp.where(departed, 0.0, state)
    return (final_state, arrived)


def solution(mesh):
    placed = (
        P(None, "wide", "cross"),
        P("wide", "cross"),
        P(None, "wide", "cross"),
        P("wide", "cross", None),
    )
    return jax.shard_map(
        local,
        mesh=mesh,
        in_specs=placed,
        out_specs=(P(None, "wide", "cross"), P(None, "wide", "cross")),
        check_vma=False,
    )
```

profile of v0, /device:TPU:57, one launch (start us, length us, event | category | flops | bytes accessed | tf_op | source)
XLA Modules:
  0.0 258.3 jit_solution(12291778425367433831)
XLA Ops:
  1.8 1.7 fusion.187
  4.5 1.7 fusion.194
  24.9 4.9 %collective-permute-start = (f32[19,1,16,32]{3,2,0,1:T(8,128)S(1)}, f32[19,1,16,32]{3,2,0,1:T(8,128)S(1)}, u32[]{:S(2)}, u32[]{:S(2)}) collective-permute-start(f32[19,1,16,32]{3,2,0,1:T(8,128)S(1)} %get-tuple-element.124), channel_id=1, source_target_pairs={{0,16},{16,32},{32,48},{48,64},{64,80},{80,96},{96,112},{112,128},... | collective-permute-start | bytes 116744 | tf_op jit(solution)/shard_map/ppermute | solution.py:41
  29.8 14.0 %collective-permute-start.1 = (f32[19,1,16,32]{3,2,0,1:T(8,128)S(1)}, f32[19,1,16,32]{3,2,0,1:T(8,128)S(1)}, u32[]{:S(2)}, u32[]{:S(2)}) collective-permute-start(f32[19,1,16,32]{3,2,0,1:T(8,128)S(1)} %get-tuple-element.125), channel_id=1, source_target_pairs={{16,0},{32,16},{48,32},{64,48},{80,64},{96,80},{112,96},{128,112},... | collective-permute-start | bytes 116744 | tf_op jit(solution)/shard_map/ppermute | solution.py:44
  43.9 1.8 collective-permute-done
  46.8 6.0 %collective-permute-start.2 = (f32[19,18,1,32]{3,2,0,1:T(1,128)S(1)}, f32[19,18,1,32]{3,2,0,1:T(1,128)S(1)}, u32[]{:S(2)}, u32[]{:S(2)}) collective-permute-start(f32[19,18,1,32]{3,2,0,1:T(1,128)S(1)} %get-tuple-element.116), channel_id=1, source_target_pairs={{0,1},{1,2},{2,3},{3,4},{4,5},{5,6},{6,7},{7,8},{8,9},{9,10},{10,1... | collective-permute-start | bytes 131336 | tf_op jit(solution)/shard_map/ppermute | solution.py:41
  52.8 1.9 collective-permute-start.3
  55.2 5.6 %collective-permute-done.3 = f32[19,18,1,32]{3,2,0,1:T(1,128)S(1)} collective-permute-done((f32[19,18,1,32]{3,2,0,1:T(1,128)S(1)}, f32[19,18,1,32]{3,2,0,1:T(1,128)S(1)}, u32[]{:S(2)}, u32[]{:S(2)}) %collective-permute-start.3) | collective-permute-done | bytes 43808 | tf_op jit(solution)/shard_map/ppermute | solution.py:44
  60.8 3.0 %pad_maximum_fusion = f32[19,18,18,32]{3,2,0,1:T(8,128)} fusion(f32[19,18,1,32]{3,2,0,1:T(1,128)S(1)} %collective-permute-done.3, f32[19,1,16,32]{3,2,0,1:T(8,128)S(1)} %collective-permute-done.1, f32[19,16,16,32]{3,2,0,1:T(8,128)S(1)} %constant_dynamic-update-slice_fusion, f32[19,1,16,32]{3,2,0,1:T(8,128)S(1)} %collective-permute-done, ...), kind=kLoop, calls=%fused_computation | loop fusion | flops 787968 | bytes 1575936 | tf_op jit(solution)/shard_map/concatenate | solution.py:45
  63.9 3.3 %reshape.376 = f32[19,18,576]{2,0,1:T(8,128)S(1)} reshape(f32[19,18,18,32]{3,2,0,1:T(8,128)} %pad_maximum_fusion) | data formatting | bytes 1575936 | tf_op jit(solution)/shard_map/reshape | solution.py:117
  89.5 1.9 collective-permute-start.4
  91.4 7.4 %collective-permute-start.5 = (f32[19,1,16,32]{3,2,0,1:T(8,128)S(1)}, f32[19,1,16,32]{3,2,0,1:T(8,128)S(1)}, u32[]{:S(2)}, u32[]{:S(2)}) collective-permute-start(f32[19,1,16,32]{3,2,0,1:T(8,128)S(1)} %get-tuple-element.123), channel_id=1, source_target_pairs={{16,0},{32,16},{48,32},{64,48},{80,64},{96,80},{112,96},{128,112},... | collective-permute-start | bytes 116744 | tf_op jit(solution)/shard_map/ppermute | solution.py:44
  99.5 1.5 collective-permute-done.5
  101.3 3.2 %collective-permute-start.6 = (f32[19,18,1,32]{3,2,0,1:T(1,128)S(1)}, f32[19,18,1,32]{3,2,0,1:T(1,128)S(1)}, u32[]{:S(2)}, u32[]{:S(2)}) collective-permute-start(f32[19,18,1,32]{3,2,0,1:T(1,128)S(1)} %get-tuple-element.114), channel_id=1, source_target_pairs={{0,1},{1,2},{2,3},{3,4},{4,5},{5,6},{6,7},{7,8},{8,9},{9,10},{10,1... | collective-permute-start | bytes 131336 | tf_op jit(solution)/shard_map/ppermute | solution.py:41
  104.5 2.1 collective-permute-start.7
  106.9 5.6 %collective-permute-done.7 = f32[19,18,1,32]{3,2,0,1:T(1,128)S(1)} collective-permute-done((f32[19,18,1,32]{3,2,0,1:T(1,128)S(1)}, f32[19,18,1,32]{3,2,0,1:T(1,128)S(1)}, u32[]{:S(2)}, u32[]{:S(2)}) %collective-permute-start.7) | collective-permute-done | bytes 43808 | tf_op jit(solution)/shard_map/ppermute | solution.py:44
  112.5 3.0 %pad_maximum_fusion.1 = f32[19,18,18,32]{3,2,0,1:T(8,128)} fusion(f32[19,18,1,32]{3,2,0,1:T(1,128)S(1)} %collective-permute-done.7, f32[19,1,16,32]{3,2,0,1:T(8,128)S(1)} %collective-permute-done.5, f32[19,16,16,32]{3,2,0,1:T(8,128)S(1)} %constant_dynamic-update-slice_fusion.19, f32[19,1,16,32]{3,2,0,1:T(8,128)S(1)} %collective-permute-done.4, ...), kind=kLoop, calls=%fused_computation.1 | loop fusion | flops 787968 | bytes 1575936 | tf_op jit(solution)/shard_map/concatenate | solution.py:45
  115.8 3.2 %reshape.377 = f32[19,18,576]{2,0,1:T(8,128)S(1)} reshape(f32[19,18,18,32]{3,2,0,1:T(8,128)} %pad_maximum_fusion.1) | data formatting | bytes 1575936 | tf_op jit(solution)/shard_map/reshape | solution.py:117
  141.2 1.9 collective-permute-start.8
  143.1 7.4 %collective-permute-start.9 = (f32[19,1,16,32]{3,2,0,1:T(8,128)S(1)}, f32[19,1,16,32]{3,2,0,1:T(8,128)S(1)}, u32[]{:S(2)}, u32[]{:S(2)}) collective-permute-start(f32[19,1,16,32]{3,2,0,1:T(8,128)S(1)} %get-tuple-element.121), channel_id=1, source_target_pairs={{16,0},{32,16},{48,32},{64,48},{80,64},{96,80},{112,96},{128,112},... | collective-permute-start | bytes 116744 | tf_op jit(solution)/shard_map/ppermute | solution.py:44
  151.2 1.5 collective-permute-done.9
  153.0 3.0 %collective-permute-start.10 = (f32[19,18,1,32]{3,2,0,1:T(1,128)S(1)}, f32[19,18,1,32]{3,2,0,1:T(1,128)S(1)}, u32[]{:S(2)}, u32[]{:S(2)}) collective-permute-start(f32[19,18,1,32]{3,2,0,1:T(1,128)S(1)} %get-tuple-element.112), channel_id=1, source_target_pairs={{0,1},{1,2},{2,3},{3,4},{4,5},{5,6},{6,7},{7,8},{8,9},{9,10},{10,1... | collective-permute-start | bytes 131336 | tf_op jit(solution)/shard_map/ppermute | solution.py:41
  156.0 2.1 collective-permute-start.11
  161.3 2.7 %collective-permute-done.11 = f32[19,18,1,32]{3,2,0,1:T(1,128)S(1)} collective-permute-done((f32[19,18,1,32]{3,2,0,1:T(1,128)S(1)}, f32[19,18,1,32]{3,2,0,1:T(1,128)S(1)}, u32[]{:S(2)}, u32[]{:S(2)}) %collective-permute-start.11) | collective-permute-done | bytes 43808 | tf_op jit(solution)/shard_map/ppermute | solution.py:44
  164.0 3.0 %pad_maximum_fusion.2 = f32[19,18,18,32]{3,2,0,1:T(8,128)} fusion(f32[19,18,1,32]{3,2,0,1:T(1,128)S(1)} %collective-permute-done.11, f32[19,1,16,32]{3,2,0,1:T(8,128)S(1)} %collective-permute-done.9, f32[19,16,16,32]{3,2,0,1:T(8,128)S(1)} %constant_dynamic-update-slice_fusion.38, f32[19,1,16,32]{3,2,0,1:T(8,128)S(1)} %collective-permute-done.8, ...), kind=kLoop, calls=%fused_computation.2 | loop fusion | flops 787968 | bytes 1575936 | tf_op jit(solution)/shard_map/concatenate | solution.py:45
  167.0 3.2 %reshape.378 = f32[19,18,576]{2,0,1:T(8,128)S(1)} reshape(f32[19,18,18,32]{3,2,0,1:T(8,128)} %pad_maximum_fusion.2) | data formatting | bytes 1575936 | tf_op jit(solution)/shard_map/reshape | solution.py:117
  170.2 1.9 fusion.599
  177.6 1.5 stack.404
  181.3 1.5 stack.405
  185.0 1.5 stack.406
  187.9 1.5 stack.407
  190.8 1.5 stack.408
  193.7 1.5 stack.409
  196.7 1.5 stack.410
  200.3 1.5 stack.411
  204.1 1.5 stack.412
  207.8 1.5 stack.413
  211.5 1.5 stack.414
  215.2 1.5 stack.415
  219.0 1.5 stack.416
  222.6 1.5 stack.417
  233.4 1.5 copy-done
  234.9 4.0 %dynamic-slice_select_fusion = (f32[19,16,16,16]{3,2,1,0:T(8,128)S(1)}, f32[19,16,16,16]{3,2,1,0:T(8,128)}) fusion(f32[19,16,16,32]{3,2,1,0:T(8,128)} %copy-done, s32[]{:T(128)S(6)} %select_n.931, pred[]{:T(512)} %bitcast.174, pred[]{:T(512)} %bitcast.173), kind=kLoop, calls=%fused_computation.3 | loop fusion | flops 155648 | bytes 933894 | tf_op jit(solution)/shard_map/jit(_where)/select_n | solution.py:126
  238.8 3.2 %select_n.933 = f32[19,16,256]{2,1,0:T(8,128)} reshape(f32[19,16,16,16]{3,2,1,0:T(8,128)} %get-tuple-element.119) | data formatting | bytes 622592 | tf_op jit(solution)/shard_map/jit(_where)/select_n | solution.py:125
  242.1 1.9 collective-permute-start.12
  244.0 1.8 select_n.936
  245.7 7.4 %collective-permute-start.13 = (f32[19,16,256]{2,1,0:T(8,128)}, f32[19,16,256]{2,1,0:T(8,128)S(1)}, u32[]{:S(2)}, u32[]{:S(2)}) collective-permute-start(f32[19,16,256]{2,1,0:T(8,128)} %select_n.936), channel_id=1, source_target_pairs={{16,0},{32,16},{48,32},{64,48},{80,64},{96,80},{112,96},{128,112},... | collective-permute-start | bytes 933896 | tf_op jit(solution)/shard_map/ppermute | solution.py:52
  254.6 3.0 %collective-permute-done.13 = f32[19,16,256]{2,1,0:T(8,128)S(1)} collective-permute-done((f32[19,16,256]{2,1,0:T(8,128)}, f32[19,16,256]{2,1,0:T(8,128)S(1)}, u32[]{:S(2)}, u32[]{:S(2)}) %collective-permute-start.13) | collective-permute-done | bytes 311328 | tf_op jit(solution)/shard_map/ppermute | solution.py:52
  (488 shorter events, 110.1 us)
Async XLA Ops:
  4.4 10.8 %copy-start.15 = (f32[16,512]{1,0:T(8,128)}, f32[16,512]{1,0:T(8,128)S(1)}, u32[]{:S(2)}) copy-start(f32[16,512]{1,0:T(8,128)S(1)} %get-tuple-element.204) | copy-start | bytes 98308
  4.4 10.8 %copy-start.17 = (f32[16,512]{1,0:T(8,128)}, f32[16,512]{1,0:T(8,128)S(1)}, u32[]{:S(2)}) copy-start(f32[16,512]{1,0:T(8,128)S(1)} %get-tuple-element.207) | copy-start | bytes 98308
  4.5 10.8 %copy-start.19 = (f32[16,512]{1,0:T(8,128)}, f32[16,512]{1,0:T(8,128)S(1)}, u32[]{:S(2)}) copy-start(f32[16,512]{1,0:T(8,128)S(1)} %get-tuple-element.208) | copy-start | bytes 98308
  4.5 10.8 %copy-start.21 = (f32[16,512]{1,0:T(8,128)}, f32[16,512]{1,0:T(8,128)S(1)}, u32[]{:S(2)}) copy-start(f32[16,512]{1,0:T(8,128)S(1)} %get-tuple-element.209) | copy-start | bytes 98308
  6.2 8.7 %copy-start.35 = (f32[16,512]{1,0:T(8,128)}, f32[16,512]{1,0:T(8,128)S(1)}, u32[]{:S(2)}) copy-start(f32[16,512]{1,0:T(8,128)S(1)} %get-tuple-element.197) | copy-start | bytes 98308
  6.2 8.7 %copy-start.37 = (f32[16,512]{1,0:T(8,128)}, f32[16,512]{1,0:T(8,128)S(1)}, u32[]{:S(2)}) copy-start(f32[16,512]{1,0:T(8,128)S(1)} %get-tuple-element.198) | copy-start | bytes 98308
  6.2 8.7 %copy-start.39 = (f32[16,512]{1,0:T(8,128)}, f32[16,512]{1,0:T(8,128)S(1)}, u32[]{:S(2)}) copy-start(f32[16,512]{1,0:T(8,128)S(1)} %get-tuple-element.199) | copy-start | bytes 98308
  6.2 8.7 %copy-start.41 = (f32[16,512]{1,0:T(8,128)}, f32[16,512]{1,0:T(8,128)S(1)}, u32[]{:S(2)}) copy-start(f32[16,512]{1,0:T(8,128)S(1)} %get-tuple-element.200) | copy-start | bytes 98308
  6.2 8.8 %copy-start.27 = (f32[16,512]{1,0:T(8,128)}, f32[16,512]{1,0:T(8,128)S(1)}, u32[]{:S(2)}) copy-start(f32[16,512]{1,0:T(8,128)S(1)} %get-tuple-element.185) | copy-start | bytes 98308
  6.3 8.8 %copy-start.29 = (f32[16,512]{1,0:T(8,128)}, f32[16,512]{1,0:T(8,128)S(1)}, u32[]{:S(2)}) copy-start(f32[16,512]{1,0:T(8,128)S(1)} %get-tuple-element.194) | copy-start | bytes 98308
  6.3 8.8 %copy-start.31 = (f32[16,512]{1,0:T(8,128)}, f32[16,512]{1,0:T(8,128)S(1)}, u32[]{:S(2)}) copy-start(f32[16,512]{1,0:T(8,128)S(1)} %get-tuple-element.195) | copy-start | bytes 98308
  6.3 8.8 %copy-start.33 = (f32[16,512]{1,0:T(8,128)}, f32[16,512]{1,0:T(8,128)S(1)}, u32[]{:S(2)}) copy-start(f32[16,512]{1,0:T(8,128)S(1)} %get-tuple-element.196) | copy-start | bytes 98308
  6.3 14.7 %copy-start.23 = (f32[16,512]{1,0:T(8,128)}, f32[16,512]{1,0:T(8,128)S(1)}, u32[]{:S(2)}) copy-start(f32[16,512]{1,0:T(8,128)S(1)} %get-tuple-element.183) | copy-start | bytes 98308
  6.3 8.8 %copy-start.25 = (f32[16,512]{1,0:T(8,128)S(1)}, f32[16,512]{1,0:T(8,128)}, u32[]{:S(2)}) copy-start(f32[16,512]{1,0:T(8,128)} %get-tuple-element.184) | copy-start | bytes 98308
  6.4 8.9 %copy-start.104 = (f32[16,512]{1,0:T(8,128)S(1)}, f32[16,512]{1,0:T(8,128)}, u32[]{:S(2)}) copy-start(f32[16,512]{1,0:T(8,128)} %get-tuple-element.106) | copy-start | bytes 98308
  15.5 9.2 %copy-start.12 = (f32[1,16,16,32]{3,2,1,0:T(8,128)S(1)}, f32[1,16,16,32]{3,2,1,0:T(8,128)}, u32[]{:S(2)}) copy-start(f32[1,16,16,32]{3,2,1,0:T(8,128)} %stack.331) | copy-start | bytes 98308
  24.9 20.7 %collective-permute-start = (f32[19,1,16,32]{3,2,0,1:T(8,128)S(1)}, f32[19,1,16,32]{3,2,0,1:T(8,128)S(1)}, u32[]{:S(2)}, u32[]{:S(2)}) collective-permute-start(f32[19,1,16,32]{3,2,0,1:T(8,128)S(1)} %get-tuple-element.124), channel_id=1, source_target_pairs={{0,16},{16,32},{32,48},{48,64},{64,80},{80,96},{96,112},{112,128},... | collective-permute-start | bytes 116744 | tf_op jit(solution)/shard_map/ppermute | solution.py:41
  29.8 16.7 %collective-permute-start.1 = (f32[19,1,16,32]{3,2,0,1:T(8,128)S(1)}, f32[19,1,16,32]{3,2,0,1:T(8,128)S(1)}, u32[]{:S(2)}, u32[]{:S(2)}) collective-permute-start(f32[19,1,16,32]{3,2,0,1:T(8,128)S(1)} %get-tuple-element.125), channel_id=1, source_target_pairs={{16,0},{32,16},{48,32},{64,48},{80,64},{96,80},{112,96},{128,112},... | collective-permute-start | bytes 116744 | tf_op jit(solution)/shard_map/ppermute | solution.py:44
  46.8 8.4 %collective-permute-start.2 = (f32[19,18,1,32]{3,2,0,1:T(1,128)S(1)}, f32[19,18,1,32]{3,2,0,1:T(1,128)S(1)}, u32[]{:S(2)}, u32[]{:S(2)}) collective-permute-start(f32[19,18,1,32]{3,2,0,1:T(1,128)S(1)} %get-tuple-element.116), channel_id=1, source_target_pairs={{0,1},{1,2},{2,3},{3,4},{4,5},{5,6},{6,7},{7,8},{8,9},{9,10},{10,1... | collective-permute-start | bytes 131336 | tf_op jit(solution)/shard_map/ppermute | solution.py:41
  52.8 8.0 %collective-permute-start.3 = (f32[19,18,1,32]{3,2,0,1:T(1,128)S(1)}, f32[19,18,1,32]{3,2,0,1:T(1,128)S(1)}, u32[]{:S(2)}, u32[]{:S(2)}) collective-permute-start(f32[19,18,1,32]{3,2,0,1:T(1,128)S(1)} %get-tuple-element.117), channel_id=1, source_target_pairs={{1,0},{2,1},{3,2},{4,3},{5,4},{6,5},{7,6},{8,7},{9,8},{10,9},{11,1... | collective-permute-start | bytes 131336 | tf_op jit(solution)/shard_map/ppermute | solution.py:44
  71.6 8.7 %copy-start.69 = (f32[16,512]{1,0:T(8,128)}, f32[16,512]{1,0:T(8,128)S(1)}, u32[]{:S(2)}) copy-start(f32[16,512]{1,0:T(8,128)S(1)} %get-tuple-element.251) | copy-start | bytes 98308
  71.6 8.8 %copy-start.53 = (f32[16,512]{1,0:T(8,128)}, f32[16,512]{1,0:T(8,128)S(1)}, u32[]{:S(2)}) copy-start(f32[16,512]{1,0:T(8,128)S(1)} %get-tuple-element.243) | copy-start | bytes 98308
  71.6 8.8 %copy-start.55 = (f32[16,512]{1,0:T(8,128)}, f32[16,512]{1,0:T(8,128)S(1)}, u32[]{:S(2)}) copy-start(f32[16,512]{1,0:T(8,128)S(1)} %get-tuple-element.244) | copy-start | bytes 98308
  71.6 8.8 %copy-start.57 = (f32[16,512]{1,0:T(8,128)}, f32[16,512]{1,0:T(8,128)S(1)}, u32[]{:S(2)}) copy-start(f32[16,512]{1,0:T(8,128)S(1)} %get-tuple-element.245) | copy-start | bytes 98308
  71.6 8.8 %copy-start.61 = (f32[16,512]{1,0:T(8,128)}, f32[16,512]{1,0:T(8,128)S(1)}, u32[]{:S(2)}) copy-start(f32[16,512]{1,0:T(8,128)S(1)} %get-tuple-element.247) | copy-start | bytes 98308
  71.6 9.1 %copy-start.47 = (f32[16,512]{1,0:T(8,128)}, f32[16,512]{1,0:T(8,128)S(1)}, u32[]{:S(2)}) copy-start(f32[16,512]{1,0:T(8,128)S(1)} %get-tuple-element.222) | copy-start | bytes 98308
  71.6 9.1 %copy-start.51 = (f32[16,512]{1,0:T(8,128)}, f32[16,512]{1,0:T(8,128)S(1)}, u32[]{:S(2)}) copy-start(f32[16,512]{1,0:T(8,128)S(1)} %get-tuple-element.224) | copy-start | bytes 98308
  71.6 9.1 %copy-start.59 = (f32[16,512]{1,0:T(8,128)}, f32[16,512]{1,0:T(8,128)S(1)}, u32[]{:S(2)}) copy-start(f32[16,512]{1,0:T(8,128)S(1)} %get-tuple-element.246) | copy-start | bytes 98308
  71.8 8.7 %copy-start.73 = (f32[16,512]{1,0:T(8,128)}, f32[16,512]{1,0:T(8,128)S(1)}, u32[]{:S(2)}) copy-start(f32[16,512]{1,0:T(8,128)S(1)} %get-tuple-element.253) | copy-start | bytes 98308
  71.8 8.7 %copy-start.75 = (f32[16,512]{1,0:T(8,128)}, f32[16,512]{1,0:T(8,128)S(1)}, u32[]{:S(2)}) copy-start(f32[16,512]{1,0:T(8,128)S(1)} %get-tuple-element.257) | copy-start | bytes 98308
  71.8 8.7 %copy-start.77 = (f32[16,512]{1,0:T(8,128)}, f32[16,512]{1,0:T(8,128)S(1)}, u32[]{:S(2)}) copy-start(f32[16,512]{1,0:T(8,128)S(1)} %get-tuple-element.258) | copy-start | bytes 98308
  71.9 8.7 %copy-start.79 = (f32[16,512]{1,0:T(8,128)}, f32[16,512]{1,0:T(8,128)S(1)}, u32[]{:S(2)}) copy-start(f32[16,512]{1,0:T(8,128)S(1)} %get-tuple-element.259) | copy-start | bytes 98308
  71.9 8.9 %copy-start.71 = (f32[16,512]{1,0:T(8,128)}, f32[16,512]{1,0:T(8,128)S(1)}, u32[]{:S(2)}) copy-start(f32[16,512]{1,0:T(8,128)S(1)} %get-tuple-element.252) | copy-start | bytes 98308
  71.9 8.9 %copy-start.49 = (f32[16,512]{1,0:T(8,128)S(1)}, f32[16,512]{1,0:T(8,128)}, u32[]{:S(2)}) copy-start(f32[16,512]{1,0:T(8,128)} %get-tuple-element.223) | copy-start | bytes 98308
  89.5 10.0 %collective-permute-start.4 = (f32[19,1,16,32]{3,2,0,1:T(8,128)S(1)}, f32[19,1,16,32]{3,2,0,1:T(8,128)S(1)}, u32[]{:S(2)}, u32[]{:S(2)}) collective-permute-start(f32[19,1,16,32]{3,2,0,1:T(8,128)S(1)} %get-tuple-element.122), channel_id=1, source_target_pairs={{0,16},{16,32},{32,48},{48,64},{64,80},{80,96},{96,112},{112,128},... | collective-permute-start | bytes 116744 | tf_op jit(solution)/shard_map/ppermute | solution.py:41
  91.4 9.6 %collective-permute-start.5 = (f32[19,1,16,32]{3,2,0,1:T(8,128)S(1)}, f32[19,1,16,32]{3,2,0,1:T(8,128)S(1)}, u32[]{:S(2)}, u32[]{:S(2)}) collective-permute-start(f32[19,1,16,32]{3,2,0,1:T(8,128)S(1)} %get-tuple-element.123), channel_id=1, source_target_pairs={{16,0},{32,16},{48,32},{64,48},{80,64},{96,80},{112,96},{128,112},... | collective-permute-start | bytes 116744 | tf_op jit(solution)/shard_map/ppermute | solution.py:44
  101.3 5.5 %collective-permute-start.6 = (f32[19,18,1,32]{3,2,0,1:T(1,128)S(1)}, f32[19,18,1,32]{3,2,0,1:T(1,128)S(1)}, u32[]{:S(2)}, u32[]{:S(2)}) collective-permute-start(f32[19,18,1,32]{3,2,0,1:T(1,128)S(1)} %get-tuple-element.114), channel_id=1, source_target_pairs={{0,1},{1,2},{2,3},{3,4},{4,5},{5,6},{6,7},{7,8},{8,9},{9,10},{10,1... | collective-permute-start | bytes 131336 | tf_op jit(solution)/shard_map/ppermute | solution.py:41
  104.5 8.0 %collective-permute-start.7 = (f32[19,18,1,32]{3,2,0,1:T(1,128)S(1)}, f32[19,18,1,32]{3,2,0,1:T(1,128)S(1)}, u32[]{:S(2)}, u32[]{:S(2)}) collective-permute-start(f32[19,18,1,32]{3,2,0,1:T(1,128)S(1)} %get-tuple-element.115), channel_id=1, source_target_pairs={{1,0},{2,1},{3,2},{4,3},{5,4},{6,5},{7,6},{8,7},{9,8},{10,9},{11,1... | collective-permute-start | bytes 131336 | tf_op jit(solution)/shard_map/ppermute | solution.py:44
  122.9 8.7 %copy-start.82 = (f32[16,512]{1,0:T(8,128)}, f32[16,512]{1,0:T(8,128)S(1)}, u32[]{:S(2)}) copy-start(f32[16,512]{1,0:T(8,128)S(1)} %get-tuple-element.212) | copy-start | bytes 98308
  122.9 8.7 %copy-start.83 = (f32[16,512]{1,0:T(8,128)}, f32[16,512]{1,0:T(8,128)S(1)}, u32[]{:S(2)}) copy-start(f32[16,512]{1,0:T(8,128)S(1)} %get-tuple-element.213) | copy-start | bytes 98308
  141.1 17.1 %copy-start.130 = (s32[1,1,2]{2,1,0:T(1,128)S(1)}, s32[1,1,2]{2,1,0:T(1,128)}, u32[]{:S(2)}) copy-start(s32[1,1,2]{2,1,0:T(1,128)} %param.7) | copy-start | bytes 28
  141.2 10.0 %collective-permute-start.8 = (f32[19,1,16,32]{3,2,0,1:T(8,128)S(1)}, f32[19,1,16,32]{3,2,0,1:T(8,128)S(1)}, u32[]{:S(2)}, u32[]{:S(2)}) collective-permute-start(f32[19,1,16,32]{3,2,0,1:T(8,128)S(1)} %get-tuple-element.120), channel_id=1, source_target_pairs={{0,16},{16,32},{32,48},{48,64},{64,80},{80,96},{96,112},{112,128},... | collective-permute-start | bytes 116744 | tf_op jit(solution)/shard_map/ppermute | solution.py:41
  143.1 9.6 %collective-permute-start.9 = (f32[19,1,16,32]{3,2,0,1:T(8,128)S(1)}, f32[19,1,16,32]{3,2,0,1:T(8,128)S(1)}, u32[]{:S(2)}, u32[]{:S(2)}) collective-permute-start(f32[19,1,16,32]{3,2,0,1:T(8,128)S(1)} %get-tuple-element.121), channel_id=1, source_target_pairs={{16,0},{32,16},{48,32},{64,48},{80,64},{96,80},{112,96},{128,112},... | collective-permute-start | bytes 116744 | tf_op jit(solution)/shard_map/ppermute | solution.py:44
  153.0 8.2 %collective-permute-start.10 = (f32[19,18,1,32]{3,2,0,1:T(1,128)S(1)}, f32[19,18,1,32]{3,2,0,1:T(1,128)S(1)}, u32[]{:S(2)}, u32[]{:S(2)}) collective-permute-start(f32[19,18,1,32]{3,2,0,1:T(1,128)S(1)} %get-tuple-element.112), channel_id=1, source_target_pairs={{0,1},{1,2},{2,3},{3,4},{4,5},{5,6},{6,7},{7,8},{8,9},{9,10},{10,1... | collective-permute-start | bytes 131336 | tf_op jit(solution)/shard_map/ppermute | solution.py:41
  156.0 8.0 %collective-permute-start.11 = (f32[19,18,1,32]{3,2,0,1:T(1,128)S(1)}, f32[19,18,1,32]{3,2,0,1:T(1,128)S(1)}, u32[]{:S(2)}, u32[]{:S(2)}) collective-permute-start(f32[19,18,1,32]{3,2,0,1:T(1,128)S(1)} %get-tuple-element.113), channel_id=1, source_target_pairs={{1,0},{2,1},{3,2},{4,3},{5,4},{6,5},{7,6},{8,7},{9,8},{10,9},{11,1... | collective-permute-start | bytes 131336 | tf_op jit(solution)/shard_map/ppermute | solution.py:44
  177.6 43.7 %copy-start.14 = (f32[16,512]{1,0:T(8,128)S(1)}, f32[16,512]{1,0:T(8,128)}, u32[]{:S(2)}) copy-start(f32[16,512]{1,0:T(8,128)} %get-tuple-element.40) | copy-start | bytes 98308
  242.1 12.6 %collective-permute-start.12 = (f32[19,16,256]{2,1,0:T(8,128)}, f32[19,16,256]{2,1,0:T(8,128)S(1)}, u32[]{:S(2)}, u32[]{:S(2)}) collective-permute-start(f32[19,16,256]{2,1,0:T(8,128)} %select_n.933), channel_id=1, source_target_pairs={{0,16},{16,32},{32,48},{48,64},{64,80},{80,96},{96,112},{112,128},... | collective-permute-start | bytes 933896 | tf_op jit(solution)/shard_map/ppermute | solution.py:52
  245.7 11.8 %collective-permute-start.13 = (f32[19,16,256]{2,1,0:T(8,128)}, f32[19,16,256]{2,1,0:T(8,128)S(1)}, u32[]{:S(2)}, u32[]{:S(2)}) collective-permute-start(f32[19,16,256]{2,1,0:T(8,128)} %select_n.936), channel_id=1, source_target_pairs={{16,0},{32,16},{48,32},{64,48},{80,64},{96,80},{112,96},{128,112},... | collective-permute-start | bytes 933896 | tf_op jit(solution)/shard_map/ppermute | solution.py:52
  (97 other events, 590.1 us)
where the time goes:
time: 263 us; the launch traced here: 258 us
  local copies, waits for them, and re-layouts  113 us (43%)
  starting transfers between devices  65.2 us (25%)
  other arithmetic  50 us (19%)
  waiting for transfers between devices  24 us (9%)
  between operations  5.87 us (2%)
    unnamed x354, local copies, waits for them, and re-layouts  42.7 us
    ppermute x6, starting transfers between devices, extended(): lax.ppermute(lax.slice_in_dim(block, 0, width, axis=dim), axis, backward)  35 us
    another operation x60, local copies, waits for them, and re-layouts, collide(): return jnp.stack(result)  26.9 us
    another operation x20, local copies, waits for them, and re-layouts, stream(): return jnp.stack(result)  22.9 us
    unnamed x18, other arithmetic  22.5 us
    ppermute x6, starting transfers between devices, extended(): lax.ppermute(lax.slice_in_dim(block, block.shape[dim] - width, None, axis...  20.8 us
    ppermute x6, waiting for transfers between devices, extended(): lax.ppermute(lax.slice_in_dim(block, 0, width, axis=dim), axis, backward)  17.7 us
    reshape x3, local copies, waits for them, and re-layouts, local(): padded = framed.reshape(19, rows + 2, (height + 2) * depth)  9.8 us
  transfers between devices with their start and end apart: 14, of which 11 were waited for; matrix products, arithmetic and copies ran while one was open for 2% of the time, Pallas kernels for 0%

commit v1 on v0

v1 whole, which is shorter than its diff:
```python
import jax
import jax.numpy as jnp
from jax import lax
from jax.experimental import pallas as pl
from jax.experimental.pallas import tpu as pltpu
from jax.sharding import PartitionSpec as P

MESH = pl.DeviceIdType.MESH
BLOCK = 16
DEPTH = 32
STEPS = 3
ROWS = 16
SPAN = 512
LANES = 128

VELOCITY = (
    (0, 0, 0),
    (1, 0, 0),
    (-1, 0, 0),
    (0, 1, 0),
    (0, -1, 0),
    (0, 0, 1),
    (0, 0, -1),
    (1, 1, 0),
    (-1, -1, 0),
    (1, -1, 0),
    (-1, 1, 0),
    (1, 0, 1),
    (-1, 0, -1),
    (1, 0, -1),
    (-1, 0, 1),
    (0, 1, 1),
    (0, -1, -1),
    (0, 1, -1),
    (0, -1, 1),
)
OPPOSITE = (0, 2, 1, 4, 3, 6, 5, 8, 7, 10, 9, 12, 11, 14, 13, 16, 15, 18, 17)
PAIRS = tuple((q, q + 1) for q in range(1, 19, 2))
CROSS_X = ((1, 7, 9, 11, 13), (2, 8, 10, 12, 14))
CROSS_Y = ((3, 7, 10, 15, 17), (4, 8, 9, 16, 18))
SIGN = (1, -1)
TILES = tuple((q, row, col) for q in range(19) for row in range(2) for col in range(2))


def touched(tile):
    q, row, col = tile
    step_x, step_y, _ = VELOCITY[q]
    return step_x == 1 - 2 * row or step_y == 1 - 2 * col


EARLY = tuple(t for t in TILES if not touched(t))
LATE = tuple(t for t in TILES if touched(t))
ORDER = EARLY + LATE
PLACE = {t: i for i, t in enumerate(ORDER)}


def blocked_bits(flags, q, rows, lanes):
    plane, bit = (0, q) if q < 10 else (1, q - 10)
    return jnp.bitwise_and(flags[plane, rows, lanes], 1 << bit) != 0


def collide(state, relax, post):
    def group(number, carry):
        rows = pl.ds(pl.multiple_of((number // 4) * 8, 8), 8)
        lanes = pl.ds(pl.multiple_of((number % 4) * LANES, LANES), LANES)
        f = [state[q, rows, lanes] for q in range(19)]
        rate = relax[rows, lanes]
        diff = {a: f[a] - f[b] for a, b in PAIRS}
        rho = f[0]
        for a, b in PAIRS:
            rho = rho + (f[a] + f[b])
        scale = 3.0 / rho
        ux = (diff[1] + diff[7] + diff[9] + diff[11] + diff[13]) * scale
        uy = (diff[3] + diff[7] - diff[9] + diff[15] + diff[17]) * scale
        uz = (diff[5] + diff[11] - diff[13] + diff[15] - diff[17]) * scale
        base = 1.0 - (ux * ux + uy * uy + uz * uz) * (1.0 / 6.0)
        keep = 1.0 - rate
        mass = rate * rho
        post[0, rows, lanes] = keep * f[0] + (mass * (1.0 / 3.0)) * base
        axis = mass * (1.0 / 18.0)
        edge = mass * (1.0 / 36.0)
        for a, b in PAIRS:
            cx, cy, cz = VELOCITY[a]
            along = None
            for c, u in ((cx, ux), (cy, uy), (cz, uz)):
                if c != 0:
                    along = u if along is None else (along + u if c > 0 else along - u)
            weight = axis if a < 7 else edge
            even = weight * (base + 0.5 * (along * along))
            odd = weight * along
            post[a, rows, lanes] = keep * f[a] + (even + odd)
            post[b, rows, lanes] = keep * f[b] + (even - odd)
        return carry

    lax.fori_loop(0, 8, group, 0)


def rolled(value, amount, axis):
    amount = amount % value.shape[axis]
    return value if amount == 0 else pltpu.roll(value, amount, axis)


def kernel(
    populations, relaxation, link_flags, migrations, final, guest,
    state, post, relax, flags,
    x_out, x_in, y_out, y_in, c_in,
    east_out, west_out, east_in, west_in,
    load_sem, halo_send, halo_recv, move_send, move_recv,
):
    w = lax.axis_index("wide")
    k = lax.axis_index("cross")
    n_wide = lax.axis_size("wide")
    n_cross = lax.axis_size("cross")
    wide = (lax.rem(w + 1, n_wide), lax.rem(w + n_wide - 1, n_wide))
    cross = (lax.rem(k + 1, n_cross), lax.rem(k + n_cross - 1, n_cross))
    partners = [(wide[0], k), (wide[1], k), (w, cross[0]), (w, cross[1])]
    partners += [(wide[i], cross[j]) for i in range(2) for j in range(2)]

    loads = [
        pltpu.make_async_copy(populations, state, load_sem.at[0]),
        pltpu.make_async_copy(relaxation, relax, load_sem.at[1]),
        pltpu.make_async_copy(link_flags, flags, load_sem.at[2]),
    ]
    for load in loads:
        load.start()
    barrier = pltpu.get_barrier_semaphore()
    for partner in partners:
        pl.semaphore_signal(barrier, inc=1, device_id=partner, device_id_type=MESH)
    for load in loads:
        load.wait()

    lane = lax.broadcasted_iota(jnp.int32, (ROWS, LANES), 1)
    line = lax.broadcasted_iota(jnp.int32, (8, SPAN), 0)
    corner_lane = lax.broadcasted_iota(jnp.int32, (1, SPAN), 1)
    chosen = migrations[0, 0, 0]
    heading = migrations[0, 0, 1]
    whole = slice(None)

    def sends(step):
        copies = []
        for i in range(2):
            copies.append((x_out.at[step, i], x_in.at[step, i]))
        for i in range(2):
            copies.append((y_out.at[step, i], y_in.at[step, i]))
        for i in range(2):
            for j in range(2):
                lanes = pl.ds(0 if j == 0 else SPAN - LANES, LANES)
                copies.append((x_out.at[step, i, :, lanes], c_in.at[step, 2 * i + j]))
        return [
            pltpu.make_async_remote_copy(
                src_ref=source,
                dst_ref=target,
                send_sem=halo_send.at[step, number],
                recv_sem=halo_recv.at[step, number],
                device_id=partners[number],
                device_id_type=MESH,
            )
            for number, (source, target) in enumerate(copies)
        ]

    def faces(step):
        for i in range(2):
            for j, q in enumerate(CROSS_X[i]):
                _, cy, cz = VELOCITY[q]
                rows = slice(8, 16) if i == 0 else slice(0, 8)
                edge = rolled(post[q, rows, :], cy * DEPTH + cz, 1)
                x_out[step, i, j : j + 1, :] = edge[7:8] if i == 0 else edge[0:1]
        for i in range(2):
            packed = [None, None]
            for j, q in enumerate(CROSS_Y[i]):
                cx, cy, cz = VELOCITY[q]
                lanes = slice(SPAN - LANES, SPAN) if i == 0 else slice(0, LANES)
                edge = rolled(post[q, :, lanes], cy * DEPTH + cz + DEPTH * j, 1)
                edge = rolled(edge, cx, 0)
                half = j // 4
                if packed[half] is None:
                    packed[half] = edge
                else:
                    first = (DEPTH * j if i == 0 else DEPTH * j + LANES - DEPTH) % LANES
                    here = (lane >= first) & (lane < first + DEPTH)
                    packed[half] = jnp.where(here, edge, packed[half])
            for half in range(2):
                y_out[step, i, half] = packed[half]

    def stream(last):
        for q in range(19):
            cx, cy, cz = VELOCITY[q]
            value = post[q]
            if q > 0:
                value = rolled(rolled(value, cy * DEPTH + cz, 1), cx, 0)
                value = jnp.where(blocked_bits(flags, q, whole, whole), post[OPPOSITE[q]], value)
            if last:
                value = jnp.where(jnp.bitwise_and(flags[0], 1) == 0, value, 0.0)
            state[q] = value

    def patch(step, last):
        for i in range(2):
            lanes = slice(0, LANES) if i == 0 else slice(SPAN - LANES, SPAN)
            here = lane < DEPTH if i == 0 else lane >= LANES - DEPTH
            for j, q in enumerate(CROSS_Y[i]):
                value = rolled(y_in[step, i, j // 4], -DEPTH * j, 1)
                keep = blocked_bits(flags, q, whole, lanes)
                if last:
                    keep = keep | (jnp.bitwise_and(flags[0, :, lanes], 1) != 0)
                state[q, :, lanes] = jnp.where(here & ~keep, value, state[q, :, lanes])
        for i in range(2):
            rows = slice(0, 8) if i == 0 else slice(8, 16)
            here = line == (0 if i == 0 else 7)
            for j, q in enumerate(CROSS_X[i]):
                value = x_in[step, i, j : j + 1, :]
                cy = VELOCITY[q][1]
                if cy != 0:
                    corner = c_in[step, 2 * i + (0 if cy > 0 else 1), j : j + 1, :]
                    corner = jnp.concatenate([corner] * (SPAN // LANES), axis=1)
                    reach = corner_lane < DEPTH if cy > 0 else corner_lane >= SPAN - DEPTH
                    value = jnp.where(reach, corner, value)
                value = jnp.broadcast_to(value, (8, SPAN))
                keep = blocked_bits(flags, q, rows, whole)
                if last:
                    keep = keep | (jnp.bitwise_and(flags[0, rows, :], 1) != 0)
                state[q, rows, :] = jnp.where(here & ~keep, value, state[q, rows, :])

    for step in range(STEPS):
        last = step == STEPS - 1
        collide(state, relax, post)
        faces(step)
        if step == 0:
            pl.semaphore_wait(barrier, len(partners))
        copies = sends(step)
        for copy in copies:
            copy.start()
        stream(last)
        if last:
            break
        for copy in copies:
            copy.wait()
        patch(step, last)

    tile_lane = lax.broadcasted_iota(jnp.int32, (8, LANES), 1)
    first_pick = (tile_lane % 64) < 16
    second_pick = tile_lane < 32

    def packed_half(q, rows, lanes):
        value = state[q, rows, lanes]
        value = jnp.where(chosen == 1, rolled(value, -BLOCK, 1), value)
        value = jnp.where(first_pick, value, rolled(value, -BLOCK, 1))
        return jnp.where(second_pick, value, rolled(value, -2 * BLOCK, 1))

    def pack(tiles):
        for tile in tiles:
            q, row, col = tile
            rows = slice(8 * row, 8 * row + 8)
            low = packed_half(q, rows, slice(2 * col * LANES, (2 * col + 1) * LANES))
            high = packed_half(q, rows, slice((2 * col + 1) * LANES, (2 * col + 2) * LANES))
            value = jnp.where(tile_lane < 64, low, rolled(high, 64, 1))
            east_out[PLACE[tile]] = jnp.where(heading == 1, value, 0.0)
            west_out[PLACE[tile]] = jnp.where(heading == -1, value, 0.0)

    def moves(part):
        span = pl.ds(0, len(EARLY)) if part == 0 else pl.ds(len(EARLY), len(LATE))
        return [
            pltpu.make_async_remote_copy(
                src_ref=source.at[span],
                dst_ref=target.at[span],
                send_sem=move_send.at[part, number],
                recv_sem=move_recv.at[part, number],
                device_id=(wide[number], k),
                device_id_type=MESH,
            )
            for number, (source, target) in enumerate(((east_out, east_in), (west_out, west_in)))
        ]

    pack(EARLY)
    early = moves(0)
    for copy in early:
        copy.start()
    for copy in copies:
        copy.wait()
    patch(STEPS - 1, True)
    pack(LATE)
    late = moves(1)
    for copy in late:
        copy.start()
    layer = (lax.broadcasted_iota(jnp.int32, (ROWS, SPAN), 1) % DEPTH) // BLOCK
    departed = (layer == chosen) & (heading != 0)
    for q in range(19):
        final[q] = jnp.where(departed, 0.0, state[q])
    for part, copies, tiles in ((0, early, EARLY), (1, late, LATE)):
        for copy in copies:
            copy.wait()
        for tile in tiles:
            q, row, col = tile
            place = PLACE[tile]
            rows = slice(8 * row, 8 * row + 8)
            lanes = slice(col * LANES, (col + 1) * LANES)
            guest[q, rows, lanes] = east_in[place] + west_in[place]


def local(populations, relaxation, link_flags, migrations):
    any_space = pl.BlockSpec(memory_space=pl.ANY)
    vmem = pl.BlockSpec(memory_space=pltpu.VMEM)
    f32 = jnp.float32
    cells = (19, ROWS, SPAN)
    block = (len(TILES), 8, LANES)
    return pl.pallas_call(
        kernel,
        out_shape=(
            jax.ShapeDtypeStruct(cells, f32),
            jax.ShapeDtypeStruct((19, ROWS, SPAN // 2), f32),
        ),
        in_specs=[any_space, any_space, any_space, pl.BlockSpec(memory_space=pltpu.SMEM)],
        out_specs=(vmem, vmem),
        scratch_shapes=[
            pltpu.VMEM(cells, f32),
            pltpu.VMEM(cells, f32),
            pltpu.VMEM((ROWS, SPAN), f32),
            pltpu.VMEM((2, ROWS, SPAN), jnp.int32),
            pltpu.VMEM((STEPS, 2, 8, SPAN), f32),
            pltpu.VMEM((STEPS, 2, 8, SPAN), f32),
            pltpu.VMEM((STEPS, 2, 2, ROWS, LANES), f32),
            pltpu.VMEM((STEPS, 2, 2, ROWS, LANES), f32),
            pltpu.VMEM((STEPS, 4, 8, LANES), f32),
            pltpu.VMEM(block, f32),
            pltpu.VMEM(block, f32),
            pltpu.VMEM(block, f32),
            pltpu.VMEM(block, f32),
            pltpu.SemaphoreType.DMA((3,)),
            pltpu.SemaphoreType.DMA((STEPS, 8)),
            pltpu.SemaphoreType.DMA((STEPS, 8)),
            pltpu.SemaphoreType.DMA((2, 2)),
            pltpu.SemaphoreType.DMA((2, 2)),
        ],
        compiler_params=pltpu.CompilerParams(
            collective_id=0, has_side_effects=True, vmem_limit_bytes=16 * 1024 * 1024
        ),
        cost_estimate=pl.CostEstimate(
            flops=5_000_000, bytes_accessed=2_000_000, transcendentals=0
        ),
    )(populations, relaxation, link_flags, migrations)


def solution(mesh):
    placed = (
        P(None, "wide", "cross"),
        P("wide", "cross"),
        P(None, "wide", "cross"),
        P("wide", "cross", None),
    )
    return jax.shard_map(
        local,
        mesh=mesh,
        in_specs=placed,
        out_specs=(P(None, "wide", "cross"), P(None, "wide", "cross")),
        check_vma=False,
    )
```

time: 263 us -> 52.6 us (0.20)
  the two profiles are of different devices: /device:TPU:57 before, /device:TPU:1 now
where the time goes in v1:
time: 52.6 us; the launch traced here: 52.3 us
  Pallas kernels  46.8 us (89%)
  local copies, waits for them, and re-layouts  4.87 us (9%)
  between operations  0.65 us (1%)
    pallas_call x1, Pallas kernels, local(): pl.pallas_call(kernel, out_shape=(jax.ShapeDtypeStruct(cells, f32), jax.S...  46.8 us
    unnamed x10, local copies, waits for them, and re-layouts  4.87 us

profile of v1, /device:TPU:1, one launch (start us, length us, event | category | flops | bytes accessed | tf_op | source)
XLA Modules:
  0.0 52.3 jit_solution(4460620770512839900)
XLA Ops:
  0.6 0.0 copy-start
  0.6 1.1 %copy-done = f32[19,16,512]{2,1,0:T(8,128)S(1)} copy-done((f32[19,16,512]{2,1,0:T(8,128)S(1)}, f32[19,16,512]{2,1,0:T(8,128)}, u32[]{:S(2)}) %copy-start) | copy-done | bytes 622616
  1.7 0.0 copy-start.1
  1.7 0.8 %copy-done.1 = s32[2,16,512]{2,1,0:T(8,128)S(1)} copy-done((s32[2,16,512]{2,1,0:T(8,128)S(1)}, s32[2,16,512]{2,1,0:T(8,128)}, u32[]{:S(2)}) %copy-start.1) | copy-done | bytes 65560
  2.5 0.0 copy-start.2
  2.5 0.8 %copy-done.2 = f32[16,512]{1,0:T(8,128)S(1)} copy-done((f32[16,512]{1,0:T(8,128)S(1)}, f32[16,512]{1,0:T(8,128)}, u32[]{:S(2)}) %copy-start.2) | copy-done | bytes 32792
  3.3 0.0 copy-start.3
  3.3 0.7 %copy-done.3 = s32[1,1,2]{2,1,0:T(1,128)S(1)} copy-done((s32[1,1,2]{2,1,0:T(1,128)S(1)}, s32[1,1,2]{2,1,0:T(1,128)}, u32[]{:S(2)}) %copy-start.3) | copy-done | bytes 32
  4.0 46.8 %shard_map.59 = (f32[19,16,512]{2,1,0:T(8,128)S(1)}, f32[19,16,256]{2,1,0:T(8,128)S(1)}) custom-call(f32[19,16,512]{2,1,0:T(8,128)S(1)} %copy-done, f32[16,512]{1,0:T(8,128)S(1)} %copy-done.2, s32[2,16,512]{2,1,0:T(8,128)S(1)} %copy-done.1, s32[1,1,2]{2,1,0:T(1,128)S(1)} %copy-done.3), custom_call_target="tpu_custom_call" | custom-call | flops 5000000 | bytes 2000000 | tf_op jit(solution)/shard_map/pallas_call | solution.py:305
  50.7 0.8 %copy.8 = f32[19,16,512]{2,1,0:T(8,128)} copy(f32[19,16,512]{2,1,0:T(8,128)S(1)} %get-tuple-element.4) | data formatting | bytes 1245184
  51.6 0.7 %copy.9 = f32[19,16,256]{2,1,0:T(8,128)} copy(f32[19,16,256]{2,1,0:T(8,128)S(1)} %get-tuple-element.5) | data formatting | bytes 622592
Async XLA Ops:
  0.6 1.1 %copy-start = (f32[19,16,512]{2,1,0:T(8,128)S(1)}, f32[19,16,512]{2,1,0:T(8,128)}, u32[]{:S(2)}) copy-start(f32[19,16,512]{2,1,0:T(8,128)} %populations.1) | copy-start | bytes 1867780
  1.7 0.8 %copy-start.1 = (s32[2,16,512]{2,1,0:T(8,128)S(1)}, s32[2,16,512]{2,1,0:T(8,128)}, u32[]{:S(2)}) copy-start(s32[2,16,512]{2,1,0:T(8,128)} %link_flags.1) | copy-start | bytes 196612
  2.5 0.8 %copy-start.2 = (f32[16,512]{1,0:T(8,128)S(1)}, f32[16,512]{1,0:T(8,128)}, u32[]{:S(2)}) copy-start(f32[16,512]{1,0:T(8,128)} %relaxation.1) | copy-start | bytes 98308
  3.3 0.7 %copy-start.3 = (s32[1,1,2]{2,1,0:T(1,128)S(1)}, s32[1,1,2]{2,1,0:T(1,128)}, u32[]{:S(2)}) copy-start(s32[1,1,2]{2,1,0:T(1,128)} %migrations.1) | copy-start | bytes 28

commit v2 on v1

v2 whole, which is shorter than its diff:
```python
import jax
import jax.numpy as jnp
from jax import lax
from jax.experimental import pallas as pl
from jax.experimental.pallas import tpu as pltpu
from jax.sharding import PartitionSpec as P

MESH = pl.DeviceIdType.MESH
BLOCK = 16
DEPTH = 32
ROWS = 16
SPAN = 512
LANES = 128
EXT_ROWS = 24
EXT_SPAN = 768
PLANES = 22
MESSAGE = 56

VELOCITY = (
    (0, 0, 0),
    (1, 0, 0),
    (-1, 0, 0),
    (0, 1, 0),
    (0, -1, 0),
    (0, 0, 1),
    (0, 0, -1),
    (1, 1, 0),
    (-1, -1, 0),
    (1, -1, 0),
    (-1, 1, 0),
    (1, 0, 1),
    (-1, 0, -1),
    (1, 0, -1),
    (-1, 0, 1),
    (0, 1, 1),
    (0, -1, -1),
    (0, 1, -1),
    (0, -1, 1),
)
OPPOSITE = (0, 2, 1, 4, 3, 6, 5, 8, 7, 10, 9, 12, 11, 14, 13, 16, 15, 18, 17)
PAIRS = tuple((q, q + 1) for q in range(1, 19, 2))
CROSS_X = ((1, 7, 9, 11, 13), (2, 8, 10, 12, 14))
CROSS_Y = ((3, 7, 10, 15, 17), (4, 8, 9, 16, 18))
SIGN = (1, -1)
PARTS = ((0, 1, 2, 3, 4), (5, 6, 7, 8, 9), (10, 11, 12, 13, 14), (15, 16, 17, 18))


def blocked_bits(flags, q, rows, lanes):
    plane, bit = (0, q) if q < 10 else (1, q - 10)
    return jnp.bitwise_and(flags[plane, rows, lanes], 1 << bit) != 0


def collide(state, relax, post, across, down):
    def group(number, carry):
        rows = pl.ds(pl.multiple_of((number // across) * 8, 8), 8)
        lanes = pl.ds(pl.multiple_of((number % across) * LANES, LANES), LANES)
        f = [state[q, rows, lanes] for q in range(19)]
        rate = relax[rows, lanes]
        diff = {a: f[a] - f[b] for a, b in PAIRS}
        rho = f[0]
        for a, b in PAIRS:
            rho = rho + (f[a] + f[b])
        scale = 3.0 / rho
        ux = (diff[1] + diff[7] + diff[9] + diff[11] + diff[13]) * scale
        uy = (diff[3] + diff[7] - diff[9] + diff[15] + diff[17]) * scale
        uz = (diff[5] + diff[11] - diff[13] + diff[15] - diff[17]) * scale
        base = 1.0 - (ux * ux + uy * uy + uz * uz) * (1.0 / 6.0)
        keep = 1.0 - rate
        mass = rate * rho
        post[0, rows, lanes] = keep * f[0] + (mass * (1.0 / 3.0)) * base
        axis = mass * (1.0 / 18.0)
        edge = mass * (1.0 / 36.0)
        for a, b in PAIRS:
            cx, cy, cz = VELOCITY[a]
            along = None
            for c, u in ((cx, ux), (cy, uy), (cz, uz)):
                if c != 0:
                    along = u if along is None else (along + u if c > 0 else along - u)
            weight = axis if a < 7 else edge
            even = weight * (base + 0.5 * (along * along))
            odd = weight * along
            post[a, rows, lanes] = keep * f[a] + (even + odd)
            post[b, rows, lanes] = keep * f[b] + (even - odd)
        return carry

    lax.fori_loop(0, across * down, group, 0)


def rolled(value, amount, axis):
    amount = amount % value.shape[axis]
    return value if amount == 0 else pltpu.roll(value, amount, axis)


def streamed(post, flags, batch, rows, lanes):
    values = [post[q] for q in batch]
    values = [
        rolled(v, VELOCITY[q][1] * DEPTH + VELOCITY[q][2], 1) for q, v in zip(batch, values)
    ]
    values = [rolled(v, VELOCITY[q][0], 0)[rows, lanes] for q, v in zip(batch, values)]
    return [
        v
        if q == 0
        else jnp.where(blocked_bits(flags, q, rows, lanes), post[OPPOSITE[q], rows, lanes], v)
        for q, v in zip(batch, values)
    ]


def kernel(
    populations, relaxation, link_flags, migrations, final, guest,
    state, post, relax, flags, move,
    x_out, x_in, c_in, y_in, y_relax, y_flags,
    east_out, west_out, east_in, west_in,
    load_sem, halo_send, halo_recv, move_send, move_recv,
):
    w = lax.axis_index("wide")
    k = lax.axis_index("cross")
    n_wide = lax.axis_size("wide")
    n_cross = lax.axis_size("cross")
    wide = (lax.rem(w + 1, n_wide), lax.rem(w + n_wide - 1, n_wide))
    cross = (lax.rem(k + 1, n_cross), lax.rem(k + n_cross - 1, n_cross))
    in_wide = (w < n_wide - 1, w > 0)
    in_cross = (k < n_cross - 1, k > 0)
    partners = [(wide[0], k), (wide[1], k), (w, cross[0]), (w, cross[1])]
    exists = [in_wide[0], in_wide[1], in_cross[0], in_cross[1]]
    for i in range(2):
        for j in range(2):
            partners.append((wide[i], cross[j]))
            exists.append(jnp.logical_and(in_wide[i], in_cross[j]))
    behind = [exists[n] for n in (1, 0, 3, 2, 7, 6, 5, 4)]

    own_rows, own_lanes = slice(0, ROWS), slice(0, SPAN)
    all_rows, all_lanes = slice(0, EXT_ROWS), slice(0, EXT_SPAN)
    loads = [
        pltpu.make_async_copy(populations, state.at[:, own_rows, own_lanes], load_sem.at[0]),
        pltpu.make_async_copy(relaxation, relax.at[own_rows, own_lanes], load_sem.at[1]),
        pltpu.make_async_copy(link_flags, flags.at[:, own_rows, own_lanes], load_sem.at[2]),
        pltpu.make_async_copy(migrations, move, load_sem.at[3]),
    ]
    for load in loads:
        load.start()
    barrier = pltpu.get_barrier_semaphore()
    for partner, there in zip(partners, exists):

        @pl.when(there)
        def _(partner=partner):
            pl.semaphore_signal(barrier, inc=1, device_id=partner, device_id_type=MESH)

    for load in loads:
        load.wait()

    def remote(source, target, number, partner):
        return pltpu.make_async_remote_copy(
            src_ref=source,
            dst_ref=target,
            send_sem=halo_send.at[number],
            recv_sem=halo_recv.at[number],
            device_id=partner,
            device_id_type=MESH,
        )

    def pack_rows(source, plane):
        x_out[0, 2 * plane : 2 * plane + 2, :] = source[ROWS - 2 : ROWS, own_lanes].astype(jnp.float32)
        x_out[1, 2 * plane : 2 * plane + 2, :] = source[0:2, own_lanes].astype(jnp.float32)

    pack_rows(relax, 19)
    pack_rows(flags.at[0], 20)
    pack_rows(flags.at[1], 21)
    collide(state, relax, post, SPAN // LANES, ROWS // 8)
    for q in range(19):
        pack_rows(post.at[q], q)
    for j in range(5):
        x_out[0, 44 + j : 45 + j, :] = post[CROSS_X[0][j], ROWS - 3 : ROWS - 2, own_lanes]
        x_out[1, 44 + j : 45 + j, :] = post[CROSS_X[1][j], 2:3, own_lanes]

    along_wide = in_wide[0].astype(jnp.int32) + in_wide[1].astype(jnp.int32)
    along_cross = in_cross[0].astype(jnp.int32) + in_cross[1].astype(jnp.int32)
    pl.semaphore_wait(barrier, along_wide + along_cross + along_wide * along_cross)

    last_lanes, first_lanes = slice(SPAN - LANES, SPAN), slice(0, LANES)
    copies = []
    for i in range(2):
        for j, lanes in enumerate((last_lanes, first_lanes)):
            n = 4 + 2 * i + j
            copies.append((n, remote(x_out.at[i, :, lanes], c_in.at[2 * i + j], n, partners[n])))
    for i in range(2):
        copies.append((i, remote(x_out.at[i], x_in.at[i], i, partners[i])))
    for j, lanes in enumerate((last_lanes, first_lanes)):
        n = 2 + j
        copies.append((n, remote(post.at[:, own_rows, lanes], y_in.at[j], n, partners[n])))
        copies.append((n, remote(relax.at[own_rows, lanes], y_relax.at[j], 8 + j, partners[n])))
        copies.append((n, remote(flags.at[:, own_rows, lanes], y_flags.at[j], 10 + j, partners[n])))
    for n, copy in copies:
        pl.when(exists[n])(copy.start)
    for n, copy in copies:
        pl.when(behind[n])(copy.wait_recv)

    for j in range(2):
        lanes = slice(EXT_SPAN - LANES, EXT_SPAN) if j == 0 else slice(SPAN, SPAN + LANES)
        for q in range(19):
            post[q, own_rows, lanes] = y_in[j, q]
        relax[own_rows, lanes] = y_relax[j]
        flags[:, own_rows, lanes] = y_flags[j]

    for i in range(2):
        rows = slice(22, 24) if i == 0 else slice(16, 18)
        third = slice(21, 22) if i == 0 else slice(18, 19)
        pieces = (
            (x_in.at[i], own_lanes),
            (c_in.at[2 * i], slice(EXT_SPAN - LANES, EXT_SPAN)),
            (c_in.at[2 * i + 1], slice(SPAN, SPAN + LANES)),
        )
        for source, lanes in pieces:
            for q in range(19):
                post[q, rows, lanes] = source[2 * q : 2 * q + 2, :]
            relax[rows, lanes] = source[38:40, :]
            for plane in range(2):
                bits = source[40 + 2 * plane : 42 + 2 * plane, :]
                flags[plane, rows, lanes] = bits.astype(jnp.int32)
            for j, q in enumerate(CROSS_X[i]):
                post[q, third, lanes] = source[44 + j : 45 + j, :]

    for n, copy in copies:
        pl.when(exists[n])(copy.wait_send)

    for _ in range(2):
        for batch in ((0,), (1, 2), (3, 4), (5, 6), (7, 8), (9, 10), (11, 12), (13, 14), (15, 16), (17, 18)):
            for q, value in zip(batch, streamed(post, flags, batch, all_rows, all_lanes)):
                state[q] = value
        collide(state, relax, post, EXT_SPAN // LANES, EXT_ROWS // 8)

    chosen = move[0, 0, 0]
    heading = move[0, 0, 1]
    tile_lane = lax.broadcasted_iota(jnp.int32, (8, LANES), 1)
    first_pick = (tile_lane % 64) < 16
    second_pick = tile_lane < 32
    layer = (lax.broadcasted_iota(jnp.int32, (ROWS, SPAN), 1) % DEPTH) // BLOCK
    departed = (layer == chosen) & (heading != 0)

    def place(q, row, col):
        return 4 * q + 2 * row + col

    def pack(batch):
        tiles = [(q, row, col) for q in batch for row in range(2) for col in range(2)]
        values = []
        for q, row, col in tiles:
            for half in range(2):
                lanes = pl.ds((2 * col + half) * LANES, LANES)
                values.append(state[q, 8 * row : 8 * row + 8, lanes])
        moved = [rolled(v, -BLOCK, 1) for v in values]
        values = [jnp.where(chosen == 1, m, v) for m, v in zip(moved, values)]
        moved = [rolled(v, -BLOCK, 1) for v in values]
        values = [jnp.where(first_pick, v, m) for m, v in zip(moved, values)]
        moved = [rolled(v, -2 * BLOCK, 1) for v in values]
        values = [jnp.where(second_pick, v, m) for m, v in zip(moved, values)]
        moved = [rolled(v, 64, 1) for v in values[1::2]]
        for tile, low, high in zip(tiles, values[::2], moved):
            value = jnp.where(tile_lane < 64, low, high)
            east_out[place(*tile)] = jnp.where(heading == 1, value, 0.0)
            west_out[place(*tile)] = jnp.where(heading == -1, value, 0.0)

    def moves(part):
        span = pl.ds(4 * PARTS[part][0], 4 * len(PARTS[part]))
        return [
            pltpu.make_async_remote_copy(
                src_ref=source.at[span],
                dst_ref=target.at[span],
                send_sem=move_send.at[part, number],
                recv_sem=move_recv.at[part, number],
                device_id=(wide[number], k),
                device_id_type=MESH,
            )
            for number, (source, target) in enumerate(((east_out, east_in), (west_out, west_in)))
        ]

    started = []
    for part, pops in enumerate(PARTS):
        for begin in range(0, len(pops), 2):
            batch = pops[begin : begin + 2]
            for q, value in zip(batch, streamed(post, flags, batch, own_rows, own_lanes)):
                solid = jnp.bitwise_and(flags[0, own_rows, own_lanes], 1) != 0
                value = jnp.where(solid, 0.0, value)
                state[q, own_rows, own_lanes] = value
                final[q] = jnp.where(departed, 0.0, value)
            pack(batch)
        started.append(moves(part))
        for number, copy in enumerate(started[-1]):
            pl.when(in_wide[number])(copy.start)
    for part, pops in enumerate(PARTS):
        for number, copy in enumerate(started[part]):
            pl.when(in_wide[1 - number])(copy.wait_recv)
        for q in pops:
            for row in range(2):
                for col in range(2):
                    east = jnp.where(in_wide[1], east_in[place(q, row, col)], 0.0)
                    west = jnp.where(in_wide[0], west_in[place(q, row, col)], 0.0)
                    guest[q, 8 * row : 8 * row + 8, col * LANES : (col + 1) * LANES] = east + west
    for pair in started:
        for number, copy in enumerate(pair):
            pl.when(in_wide[number])(copy.wait_send)


def local(populations, relaxation, link_flags, migrations):
    populations, relaxation, link_flags, migrations = (
        pltpu.with_memory_space_constraint(operand, pltpu.HBM)
        for operand in (populations, relaxation, link_flags, migrations)
    )
    hbm = pl.BlockSpec(memory_space=pltpu.HBM)
    vmem = pl.BlockSpec(memory_space=pltpu.VMEM)
    f32, i32 = jnp.float32, jnp.int32
    block = (19 * 4, 8, LANES)
    return pl.pallas_call(
        kernel,
        out_shape=(
            jax.ShapeDtypeStruct((19, ROWS, SPAN), f32),
            jax.ShapeDtypeStruct((19, ROWS, SPAN // 2), f32),
        ),
        in_specs=[hbm] * 4,
        out_specs=(vmem, vmem),
        scratch_shapes=[
            pltpu.VMEM((19, EXT_ROWS, EXT_SPAN), f32),
            pltpu.VMEM((19, EXT_ROWS, EXT_SPAN), f32),
            pltpu.VMEM((EXT_ROWS, EXT_SPAN), f32),
            pltpu.VMEM((2, EXT_ROWS, EXT_SPAN), i32),
            pltpu.SMEM((1, 1, 2), i32),
            pltpu.VMEM((2, MESSAGE, SPAN), f32),
            pltpu.VMEM((2, MESSAGE, SPAN), f32),
            pltpu.VMEM((4, MESSAGE, LANES), f32),
            pltpu.VMEM((2, 19, ROWS, LANES), f32),
            pltpu.VMEM((2, ROWS, LANES), f32),
            pltpu.VMEM((2, 2, ROWS, LANES), i32),
            pltpu.VMEM(block, f32),
            pltpu.VMEM(block, f32),
            pltpu.VMEM(block, f32),
            pltpu.VMEM(block, f32),
            pltpu.SemaphoreType.DMA((4,)),
            pltpu.SemaphoreType.DMA((12,)),
            pltpu.SemaphoreType.DMA((12,)),
            pltpu.SemaphoreType.DMA((len(PARTS), 2)),
            pltpu.SemaphoreType.DMA((len(PARTS), 2)),
        ],
        compiler_params=pltpu.CompilerParams(
            collective_id=0, has_side_effects=True, vmem_limit_bytes=24 * 1024 * 1024
        ),
        cost_estimate=pl.CostEstimate(
            flops=8_000_000, bytes_accessed=2_000_000, transcendentals=0
        ),
    )(populations, relaxation, link_flags, migrations)


def solution(mesh):
    placed = (
        P(None, "wide", "cross"),
        P("wide", "cross"),
        P(None, "wide", "cross"),
        P("wide", "cross", None),
    )
    return jax.shard_map(
        local,
        mesh=mesh,
        in_specs=placed,
        out_specs=(P(None, "wide", "cross"), P(None, "wide", "cross")),
        check_vma=False,
    )
```

time: 52.6 us -> 40 us (0.76)
  the two profiles are of different devices: /device:TPU:1 before, /device:TPU:41 now
where the time goes in v2:
time: 40 us; the launch traced here: 39.8 us
  Pallas kernels  37.6 us (94%)
  local copies, waits for them, and re-layouts  1.55 us (4%)
  between operations  0.64 us (2%)
    pallas_call x1, Pallas kernels, local(): pl.pallas_call(kernel, out_shape=(jax.ShapeDtypeStruct((19, ROWS, SPAN),...  37.6 us
    unnamed x2, local copies, waits for them, and re-layouts  1.55 us

profile of v2, /device:TPU:41, one launch (start us, length us, event | category | flops | bytes accessed | tf_op | source)
XLA Modules:
  0.0 39.8 jit_solution(10082545414894896605)
XLA Ops:
  0.6 37.6 %shard_map.59 = (f32[19,16,512]{2,1,0:T(8,128)S(1)}, f32[19,16,256]{2,1,0:T(8,128)S(1)}) custom-call(f32[19,16,512]{2,1,0:T(8,128)} %populations.1, f32[16,512]{1,0:T(8,128)} %relaxation.1, s32[2,16,512]{2,1,0:T(8,128)} %link_flags.1, s32[1,1,2]{2,1,0:T(1,128)} %migrations.1), custom_call_target="tpu_custom_call" | custom-call | flops 8000000 | bytes 2000000 | tf_op jit(solution)/shard_map/pallas_call | solution.py:311
  38.3 0.8 %copy.8 = f32[19,16,512]{2,1,0:T(8,128)} copy(f32[19,16,512]{2,1,0:T(8,128)S(1)} %get-tuple-element.4) | data formatting | bytes 1245184
  39.1 0.7 %copy.9 = f32[19,16,256]{2,1,0:T(8,128)} copy(f32[19,16,256]{2,1,0:T(8,128)S(1)} %get-tuple-element.5) | data formatting | bytes 622592

commit v3 on v2

--- a/solution.py
+++ b/solution.py
@@ -13,6 +13,7 @@
 LANES = 128
 EXT_ROWS = 24
 EXT_SPAN = 768
+NEAR_SPAN = 640
 PLANES = 22
 MESSAGE = 56
 
@@ -42,7 +43,10 @@
 CROSS_X = ((1, 7, 9, 11, 13), (2, 8, 10, 12, 14))
 CROSS_Y = ((3, 7, 10, 15, 17), (4, 8, 9, 16, 18))
 SIGN = (1, -1)
-PARTS = ((0, 1, 2, 3, 4), (5, 6, 7, 8, 9), (10, 11, 12, 13, 14), (15, 16, 17, 18))
+BATCHES = ((0,),) + PAIRS
+INNER = 4
+REST = ((0, 1), (1, 0), (1, 1))
+PARTS = ((0, 1), (2, 3, 4, 5), (6, 7, 8, 9, 10, 11), (12, 13, 14, 15, 16, 17, 18))
 
 
 def blocked_bits(flags, q, rows, lanes):
@@ -83,7 +87,7 @@
             post[b, rows, lanes] = keep * f[b] + (even - odd)
         return carry
 
-    lax.fori_loop(0, across * down, group, 0)
+    lax.fori_loop(0, across * down, group, 0, unroll=5 if across == 5 else 4)
 
 
 def rolled(value, amount, axis):
@@ -91,23 +95,34 @@
     return value if amount == 0 else pltpu.roll(value, amount, axis)
 
 
-def streamed(post, flags, batch, rows, lanes):
-    values = [post[q] for q in batch]
+def streamed(post, flags, batch, height, span, rows, lanes):
+    wide = span > lanes.stop > SPAN
+
+    def kept(value):
+        if not wide:
+            return value[rows, lanes]
+        above, below = value[rows, SPAN : SPAN + LANES], value[rows, span - LANES : span]
+        here = lax.broadcasted_iota(jnp.int32, above.shape, 1) < 2 * DEPTH
+        return jnp.concatenate([value[rows, :SPAN], jnp.where(here, above, below)], axis=1)
+
+    values = [post[q, 0:height, 0:span] for q in batch]
     values = [
         rolled(v, VELOCITY[q][1] * DEPTH + VELOCITY[q][2], 1) for q, v in zip(batch, values)
     ]
-    values = [rolled(v, VELOCITY[q][0], 0)[rows, lanes] for q, v in zip(batch, values)]
+    values = [kept(rolled(v, VELOCITY[q][0], 0)) for q, v in zip(batch, values)]
     return [
         v
         if q == 0
-        else jnp.where(blocked_bits(flags, q, rows, lanes), post[OPPOSITE[q], rows, lanes], v)
+        else jnp.where(
+            blocked_bits(flags, q, rows, lanes), kept(post[OPPOSITE[q], 0:height, 0:span]), v
+        )
         for q, v in zip(batch, values)
     ]
 
 
 def kernel(
     populations, relaxation, link_flags, migrations, final, guest,
-    state, post, relax, flags, move,
+    state, post, inner, inner_post, relax, flags, move,
     x_out, x_in, c_in, y_in, y_relax, y_flags,
     east_out, west_out, east_in, west_in,
     load_sem, halo_send, halo_recv, move_send, move_recv,
@@ -129,7 +144,7 @@
     behind = [exists[n] for n in (1, 0, 3, 2, 7, 6, 5, 4)]
 
     own_rows, own_lanes = slice(0, ROWS), slice(0, SPAN)
-    all_rows, all_lanes = slice(0, EXT_ROWS), slice(0, EXT_SPAN)
+    all_rows, near_lanes = slice(0, EXT_ROWS), slice(0, NEAR_SPAN)
     loads = [
         pltpu.make_async_copy(populations, state.at[:, own_rows, own_lanes], load_sem.at[0]),
         pltpu.make_async_copy(relaxation, relax.at[own_rows, own_lanes], load_sem.at[1]),
@@ -191,6 +206,69 @@
         copies.append((n, remote(flags.at[:, own_rows, lanes], y_flags.at[j], 10 + j, partners[n])))
     for n, copy in copies:
         pl.when(exists[n])(copy.start)
+    chosen = move[0, 0, 0]
+    heading = move[0, 0, 1]
+    tile_lane = lax.broadcasted_iota(jnp.int32, (8, LANES), 1)
+    tile_row = lax.broadcasted_iota(jnp.int32, (8, LANES), 0)
+    first_pick = (tile_lane % 64) < 16
+    second_pick = tile_lane < 32
+    layer = (lax.broadcasted_iota(jnp.int32, (ROWS, SPAN), 1) % DEPTH) // BLOCK
+    departed = (layer == chosen) & (heading != 0)
+
+    def place(q, row, col):
+        return q if (row, col) == (0, 0) else 19 + 3 * q + REST.index((row, col))
+
+    def pack(source, tiles):
+        values = []
+        for q, row, col in tiles:
+            for number in ((1, 2), (3, 0))[col]:
+                lanes = slice(number * LANES, (number + 1) * LANES)
+                values.append(source[q, 8 * row : 8 * row + 8, lanes])
+        moved = [rolled(v, -BLOCK, 1) for v in values]
+        values = [jnp.where(chosen == 1, m, v) for m, v in zip(moved, values)]
+        moved = [rolled(v, -BLOCK, 1) for v in values]
+        values = [jnp.where(first_pick, v, m) for m, v in zip(moved, values)]
+        moved = [rolled(v, -2 * BLOCK, 1) for v in values]
+        values = [jnp.where(second_pick, v, m) for m, v in zip(moved, values)]
+        moved = [rolled(v, 64, 1) for v in values[1::2]]
+        for tile, low, high in zip(tiles, values[::2], moved):
+            value = jnp.where(tile_lane < 64, low, high)
+            east_out[place(*tile)] = jnp.where(heading == 1, value, 0.0)
+            west_out[place(*tile)] = jnp.where(heading == -1, value, 0.0)
+
+    def begin(part, first, count):
+        span = pl.ds(first, count)
+        pair = [
+            pltpu.make_async_remote_copy(
+                src_ref=source.at[span],
+                dst_ref=target.at[span],
+                send_sem=move_send.at[part, number],
+                recv_sem=move_recv.at[part, number],
+                device_id=(wide[number], k),
+                device_id_type=MESH,
+            )
+            for number, (source, target) in enumerate(((east_out, east_in), (west_out, west_in)))
+        ]
+        for number, copy in enumerate(pair):
+            pl.when(in_wide[number])(copy.start)
+        return pair
+
+    def cleared(value):
+        return jnp.where(jnp.bitwise_and(flags[0, own_rows, own_lanes], 1) != 0, 0.0, value)
+
+    source = post
+    for step in range(3):
+        for batch in BATCHES:
+            values = streamed(source, flags, batch, ROWS, SPAN, own_rows, own_lanes)
+            for q, value in zip(batch, values):
+                inner[q] = value if step < 2 else rolled(cleared(value), -INNER, 0)
+        if step < 2:
+            collide(inner, relax, inner_post, SPAN // LANES, ROWS // 8)
+            source = inner_post
+    for first in range(0, 19, 10):
+        pack(inner, [(q, 0, 0) for q in range(first, min(first + 10, 19))])
+    started = [begin(0, 0, 19)]
+
     for n, copy in copies:
         pl.when(behind[n])(copy.wait_recv)
 
@@ -198,8 +276,15 @@
         lanes = slice(EXT_SPAN - LANES, EXT_SPAN) if j == 0 else slice(SPAN, SPAN + LANES)
         for q in range(19):
             post[q, own_rows, lanes] = y_in[j, q]
-        relax[own_rows, lanes] = y_relax[j]
-        flags[:, own_rows, lanes] = y_flags[j]
+    near = slice(SPAN, NEAR_SPAN)
+
+    def merged(above, below):
+        here = lax.broadcasted_iota(jnp.int32, above.shape, above.ndim - 1) < 2 * DEPTH
+        return jnp.where(here, above, below)
+
+    relax[own_rows, near] = merged(y_relax[1], y_relax[0])
+    for plane in range(2):
+        flags[plane, own_rows, near] = merged(y_flags[1, plane], y_flags[0, plane])
 
     for i in range(2):
         rows = slice(22, 24) if i == 0 else slice(16, 18)
@@ -212,91 +297,82 @@
         for source, lanes in pieces:
             for q in range(19):
                 post[q, rows, lanes] = source[2 * q : 2 * q + 2, :]
-            relax[rows, lanes] = source[38:40, :]
-            for plane in range(2):
-                bits = source[40 + 2 * plane : 42 + 2 * plane, :]
-                flags[plane, rows, lanes] = bits.astype(jnp.int32)
             for j, q in enumerate(CROSS_X[i]):
                 post[q, third, lanes] = source[44 + j : 45 + j, :]
+        pieces = (
+            (lambda part: x_in[i, part, :], own_lanes),
+            (lambda part: merged(c_in[2 * i + 1, part, :], c_in[2 * i, part, :]), near),
+        )
+        for source, lanes in pieces:
+            relax[rows, lanes] = source(slice(38, 40))
+            for plane in range(2):
+                bits = source(slice(40 + 2 * plane, 42 + 2 * plane))
+                flags[plane, rows, lanes] = bits.astype(jnp.int32)
 
     for n, copy in copies:
         pl.when(exists[n])(copy.wait_send)
 
-    for _ in range(2):
-        for batch in ((0,), (1, 2), (3, 4), (5, 6), (7, 8), (9, 10), (11, 12), (13, 14), (15, 16), (17, 18)):
-            for q, value in zip(batch, streamed(post, flags, batch, all_rows, all_lanes)):
-                state[q] = value
-        collide(state, relax, post, EXT_SPAN // LANES, EXT_ROWS // 8)
-
-    chosen = move[0, 0, 0]
-    heading = move[0, 0, 1]
-    tile_lane = lax.broadcasted_iota(jnp.int32, (8, LANES), 1)
-    first_pick = (tile_lane % 64) < 16
-    second_pick = tile_lane < 32
-    layer = (lax.broadcasted_iota(jnp.int32, (ROWS, SPAN), 1) % DEPTH) // BLOCK
-    departed = (layer == chosen) & (heading != 0)
-
-    def place(q, row, col):
-        return 4 * q + 2 * row + col
-
-    def pack(batch):
-        tiles = [(q, row, col) for q in batch for row in range(2) for col in range(2)]
-        values = []
-        for q, row, col in tiles:
-            for half in range(2):
-                lanes = pl.ds((2 * col + half) * LANES, LANES)
-                values.append(state[q, 8 * row : 8 * row + 8, lanes])
-        moved = [rolled(v, -BLOCK, 1) for v in values]
-        values = [jnp.where(chosen == 1, m, v) for m, v in zip(moved, values)]
-        moved = [rolled(v, -BLOCK, 1) for v in values]
-        values = [jnp.where(first_pick, v, m) for m, v in zip(moved, values)]
-        moved = [rolled(v, -2 * BLOCK, 1) for v in values]
-        values = [jnp.where(second_pick, v, m) for m, v in zip(moved, values)]
-        moved = [rolled(v, 64, 1) for v in values[1::2]]
-        for tile, low, high in zip(tiles, values[::2], moved):
-            value = jnp.where(tile_lane < 64, low, high)
-            east_out[place(*tile)] = jnp.where(heading == 1, value, 0.0)
-            west_out[place(*tile)] = jnp.where(heading == -1, value, 0.0)
-
-    def moves(part):
-        span = pl.ds(4 * PARTS[part][0], 4 * len(PARTS[part]))
-        return [
-            pltpu.make_async_remote_copy(
-                src_ref=source.at[span],
-                dst_ref=target.at[span],
-                send_sem=move_send.at[part, number],
-                recv_sem=move_recv.at[part, number],
-                device_id=(wide[number], k),
-                device_id_type=MESH,
-            )
-            for number, (source, target) in enumerate(((east_out, east_in), (west_out, west_in)))
-        ]
-
-    started = []
+    for span in (EXT_SPAN, NEAR_SPAN):
+        for batch in BATCHES:
+            for q, value in zip(batch, streamed(post, flags, batch, EXT_ROWS, span, all_rows, near_lanes)):
+                state[q, :, near_lanes] = value
+        collide(state, relax, post, NEAR_SPAN // LANES, EXT_ROWS // 8)
+
     for part, pops in enumerate(PARTS):
-        for begin in range(0, len(pops), 2):
-            batch = pops[begin : begin + 2]
-            for q, value in zip(batch, streamed(post, flags, batch, own_rows, own_lanes)):
-                solid = jnp.bitwise_and(flags[0, own_rows, own_lanes], 1) != 0
-                value = jnp.where(solid, 0.0, value)
-                state[q, own_rows, own_lanes] = value
+        for first in range(0, len(pops), 2):
+            batch = pops[first : first + 2]
+            values = streamed(post, flags, batch, EXT_ROWS, NEAR_SPAN, own_rows, own_lanes)
+            for q, value in zip(batch, values):
+                value = cleared(value)
                 final[q] = jnp.where(departed, 0.0, value)
-            pack(batch)
-        started.append(moves(part))
-        for number, copy in enumerate(started[-1]):
-            pl.when(in_wide[number])(copy.start)
-    for part, pops in enumerate(PARTS):
+                state[q, own_rows, own_lanes] = rolled(value, -INNER, 0)
+            pack(state, [(q, row, col) for q in batch for row, col in REST])
+        started.append(begin(1 + part, 19 + 3 * pops[0], 3 * len(pops)))
+
+    def arrived(part):
         for number, copy in enumerate(started[part]):
             pl.when(in_wide[1 - number])(copy.wait_recv)
-        for q in pops:
-            for row in range(2):
-                for col in range(2):
-                    east = jnp.where(in_wide[1], east_in[place(q, row, col)], 0.0)
-                    west = jnp.where(in_wide[0], west_in[place(q, row, col)], 0.0)
-                    guest[q, 8 * row : 8 * row + 8, col * LANES : (col + 1) * LANES] = east + west
+
+    def received(q, row, col):
+        east = jnp.where(in_wide[1], east_in[place(q, row, col)], 0.0)
+        west = jnp.where(in_wide[0], west_in[place(q, row, col)], 0.0)
+        return rolled(east + west, INNER, 0)
+
+    arrived(0)
+    for part, pops in enumerate(PARTS):
+        arrived(1 + part)
+        for first in range(0, len(pops), 2):
+            batch = pops[first : first + 2]
+            tiles = [[[received(q, row, col) for col in range(2)] for row in range(2)] for q in batch]
+            tiles = [
+                [
+                    [
+                        rolled(jnp.where(tile_row < INNER, t[1 - row][col], t[row][col]), 64, 1)
+                        for col in range(2)
+                    ]
+                    for row in range(2)
+                ]
+                for t in tiles
+            ]
+            for q, t in zip(batch, tiles):
+                for row in range(2):
+                    rows = slice(8 * row, 8 * row + 8)
+                    guest[q, rows, 0:LANES] = jnp.where(tile_lane < 64, t[row][1], t[row][0])
+                    guest[q, rows, LANES:] = jnp.where(tile_lane < 64, t[row][0], t[row][1])
     for pair in started:
         for number, copy in enumerate(pair):
             pl.when(in_wide[number])(copy.wait_send)
+
+
+def store(final, guest, final_out, guest_out, sems):
+    copies = [
+        pltpu.make_async_copy(final, final_out, sems.at[0]),
+        pltpu.make_async_copy(guest, guest_out, sems.at[1]),
+    ]
+    for copy in copies:
+        copy.start()
+    for copy in copies:
+        copy.wait()
 
 
 def local(populations, relaxation, link_flags, migrations):
@@ -308,7 +384,7 @@
     vmem = pl.BlockSpec(memory_space=pltpu.VMEM)
     f32, i32 = jnp.float32, jnp.int32
     block = (19 * 4, 8, LANES)
-    return pl.pallas_call(
+    results = pl.pallas_call(
         kernel,
         out_shape=(
             jax.ShapeDtypeStruct((19, ROWS, SPAN), f32),
@@ -317,10 +393,12 @@
         in_specs=[hbm] * 4,
         out_specs=(vmem, vmem),
         scratch_shapes=[
+            pltpu.VMEM((19, EXT_ROWS, NEAR_SPAN), f32),
             pltpu.VMEM((19, EXT_ROWS, EXT_SPAN), f32),
-            pltpu.VMEM((19, EXT_ROWS, EXT_SPAN), f32),
-            pltpu.VMEM((EXT_ROWS, EXT_SPAN), f32),
-            pltpu.VMEM((2, EXT_ROWS, EXT_SPAN), i32),
+            pltpu.VMEM((19, ROWS, SPAN), f32),
+            pltpu.VMEM((19, ROWS, SPAN), f32),
+            pltpu.VMEM((EXT_ROWS, NEAR_SPAN), f32),
+            pltpu.VMEM((2, EXT_ROWS, NEAR_SPAN), i32),
             pltpu.SMEM((1, 1, 2), i32),
             pltpu.VMEM((2, MESSAGE, SPAN), f32),
             pltpu.VMEM((2, MESSAGE, SPAN), f32),
@@ -335,8 +413,8 @@
             pltpu.SemaphoreType.DMA((4,)),
             pltpu.SemaphoreType.DMA((12,)),
             pltpu.SemaphoreType.DMA((12,)),
-            pltpu.SemaphoreType.DMA((len(PARTS), 2)),
-            pltpu.SemaphoreType.DMA((len(PARTS), 2)),
+            pltpu.SemaphoreType.DMA((1 + len(PARTS), 2)),
+            pltpu.SemaphoreType.DMA((1 + len(PARTS), 2)),
         ],
         compiler_params=pltpu.CompilerParams(
             collective_id=0, has_side_effects=True, vmem_limit_bytes=24 * 1024 * 1024
@@ -345,6 +423,14 @@
             flops=8_000_000, bytes_accessed=2_000_000, transcendentals=0
         ),
     )(populations, relaxation, link_flags, migrations)
+    return pl.pallas_call(
+        store,
+        out_shape=tuple(jax.ShapeDtypeStruct(r.shape, f32) for r in results),
+        in_specs=[vmem] * 2,
+        out_specs=(hbm, hbm),
+        scratch_shapes=[pltpu.SemaphoreType.DMA((2,))],
+        compiler_params=pltpu.CompilerParams(vmem_limit_bytes=8 * 1024 * 1024),
+    )(*results)
 
 
 def solution(mesh):

time: 40 us -> 37.6 us (0.940)
  local copies, waits for them, and re-layouts: 1.55 us -> 0 us
  Pallas kernels: 37.6 us -> 36.8 us
    pallas_call x1, Pallas kernels: 37.6 us -> 35.8 us  [local(): pl.pallas_call(kernel, out_shape=(jax.ShapeDtypeStruct((19, ROWS, SPAN),...]
    unnamed x2 -> x0, local copies, waits for them, and re-layouts: 1.55 us -> none
    pallas_call x0 -> x1, Pallas kernels: none -> 0.94 us  [local(): pl.pallas_call(store, out_shape=tuple((jax.ShapeDtypeStruct(r.shape, f32)...]
where the time goes in v3:
time: 37.6 us; the launch traced here: 37.4 us
  Pallas kernels  36.8 us (98%)
  between operations  0.64 us (2%)
    pallas_call x1, Pallas kernels, local(): pl.pallas_call(kernel, out_shape=(jax.ShapeDtypeStruct((19, ROWS, SPAN),...  35.8 us
    pallas_call x1, Pallas kernels, local(): pl.pallas_call(store, out_shape=tuple((jax.ShapeDtypeStruct(r.shape, f32)...  0.94 us

profile of v3, /device:TPU:41, one launch (start us, length us, event | category | flops | bytes accessed | tf_op | source)
XLA Modules:
  0.0 37.4 jit_solution(9791279018441152045)
XLA Ops:
  0.6 35.8 %shard_map.59 = (f32[19,16,512]{2,1,0:T(8,128)S(1)}, f32[19,16,256]{2,1,0:T(8,128)S(1)}) custom-call(f32[19,16,512]{2,1,0:T(8,128)} %populations.1, f32[16,512]{1,0:T(8,128)} %relaxation.1, s32[2,16,512]{2,1,0:T(8,128)} %link_flags.1, s32[1,1,2]{2,1,0:T(1,128)} %migrations.1), custom_call_target="tpu_custom_call" | custom-call | flops 8000000 | bytes 2000000 | tf_op jit(solution)/shard_map/pallas_call | solution.py:387
  36.5 0.9 %shard_map.60 = (f32[19,16,512]{2,1,0:T(8,128)}, f32[19,16,256]{2,1,0:T(8,128)}) custom-call(f32[19,16,512]{2,1,0:T(8,128)S(1)} %get-tuple-element.4.final, f32[19,16,256]{2,1,0:T(8,128)S(1)} %get-tuple-element.5.guest), custom_call_target="tpu_custom_call" | custom-call | tf_op jit(solution)/shard_map/pallas_call | solution.py:426

commit v4 on v3

--- a/solution.py
+++ b/solution.py
@@ -16,6 +16,7 @@
 NEAR_SPAN = 640
 PLANES = 22
 MESSAGE = 56
+CORNER = 32
 
 VELOCITY = (
     (0, 0, 0),
@@ -42,7 +43,9 @@
 PAIRS = tuple((q, q + 1) for q in range(1, 19, 2))
 CROSS_X = ((1, 7, 9, 11, 13), (2, 8, 10, 12, 14))
 CROSS_Y = ((3, 7, 10, 15, 17), (4, 8, 9, 16, 18))
-SIGN = (1, -1)
+SHARED = tuple(
+    tuple(next(n for n, q in enumerate(xs) if q in ys) for ys in CROSS_Y) for xs in CROSS_X
+)
 BATCHES = ((0,),) + PAIRS
 INNER = 4
 REST = ((0, 1), (1, 0), (1, 1))
@@ -123,7 +126,7 @@
 def kernel(
     populations, relaxation, link_flags, migrations, final, guest,
     state, post, inner, inner_post, relax, flags, move,
-    x_out, x_in, c_in, y_in, y_relax, y_flags,
+    x_out, x_in, c_out, c_in, c_rows, c_full, y_in, y_relax, y_flags,
     east_out, west_out, east_in, west_in,
     load_sem, halo_send, halo_recv, move_send, move_recv,
 ):
@@ -192,11 +195,31 @@
     pl.semaphore_wait(barrier, along_wide + along_cross + along_wide * along_cross)
 
     last_lanes, first_lanes = slice(SPAN - LANES, SPAN), slice(0, LANES)
+    def corner_lanes(j, count):
+        lane = lax.broadcasted_iota(jnp.int32, (count, LANES), 1)
+        if j == 0:
+            return lane >= 2 * DEPTH, (lane >= DEPTH) & (lane < 2 * DEPTH), DEPTH
+        return lane < 2 * DEPTH, (lane >= 2 * DEPTH) & (lane < 3 * DEPTH), -DEPTH
+
     copies = []
     for i in range(2):
         for j, lanes in enumerate((last_lanes, first_lanes)):
-            n = 4 + 2 * i + j
-            copies.append((n, remote(x_out.at[i, :, lanes], c_in.at[2 * i + j], n, partners[n])))
+            n = 2 * i + j
+            near, third, shift = corner_lanes(j, 8)
+            for m, q in enumerate(CROSS_Y[j]):
+                first = 2 * m if m < 4 else 10
+                c_rows[n, first : first + 2, :] = x_out[i, 2 * q : 2 * q + 2, lanes]
+            c_rows[n, 8:9, :] = x_out[i, 48:49, lanes]
+            c_rows[n, 12:13, :] = x_out[i, 44 + SHARED[i][j] : 45 + SHARED[i][j], lanes]
+            for block in range(0, 24, 8):
+                high = rolled(x_out[i, 24 + block : 32 + block, lanes], 2 * DEPTH, 1)
+                c_out[n, block : block + 8, :] = jnp.where(
+                    near, x_out[i, block : block + 8, lanes], high
+                )
+            c_out[n, 24:32, :] = jnp.where(
+                third, c_rows[n, 0:8, :], rolled(c_rows[n, 8:16, :], shift, 1)
+            )
+            copies.append((4 + n, remote(c_out.at[n], c_in.at[n], 4 + n, partners[4 + n])))
     for i in range(2):
         copies.append((i, remote(x_out.at[i], x_in.at[i], i, partners[i])))
     for j, lanes in enumerate((last_lanes, first_lanes)):
@@ -272,6 +295,25 @@
     for n, copy in copies:
         pl.when(behind[n])(copy.wait_recv)
 
+    for i in range(2):
+        for j in range(2):
+            n = 2 * i + j
+            shift = corner_lanes(j, 8)[2]
+            for block in range(0, 24, 8):
+                value = c_in[n, block : block + 8, :]
+                c_full[n, block : block + 8, :] = value
+                c_full[n, 24 + block : 32 + block, :] = rolled(value, 2 * DEPTH, 1)
+            c_rows[n, 8:16, :] = rolled(c_in[n, 24:32, :], -shift, 1)
+            third = corner_lanes(j, 2)[1]
+            for m, q in enumerate(CROSS_Y[j]):
+                value = c_in[n, 24 + 2 * m : 26 + 2 * m, :] if m < 4 else c_rows[n, 10:12, :]
+                rows = slice(2 * q, 2 * q + 2)
+                c_full[n, rows, :] = jnp.where(third, value, c_full[n, rows, :])
+            rows = slice(44 + SHARED[i][j], 45 + SHARED[i][j])
+            third = corner_lanes(j, 1)[1]
+            c_full[n, rows, :] = jnp.where(third, c_rows[n, 12:13, :], c_full[n, rows, :])
+            c_full[n, 48:49, :] = c_rows[n, 8:9, :]
+
     for j in range(2):
         lanes = slice(EXT_SPAN - LANES, EXT_SPAN) if j == 0 else slice(SPAN, SPAN + LANES)
         for q in range(19):
@@ -291,8 +333,8 @@
         third = slice(21, 22) if i == 0 else slice(18, 19)
         pieces = (
             (x_in.at[i], own_lanes),
-            (c_in.at[2 * i], slice(EXT_SPAN - LANES, EXT_SPAN)),
-            (c_in.at[2 * i + 1], slice(SPAN, SPAN + LANES)),
+            (c_full.at[2 * i], slice(EXT_SPAN - LANES, EXT_SPAN)),
+            (c_full.at[2 * i + 1], slice(SPAN, SPAN + LANES)),
         )
         for source, lanes in pieces:
             for q in range(19):
@@ -301,7 +343,7 @@
                 post[q, third, lanes] = source[44 + j : 45 + j, :]
         pieces = (
             (lambda part: x_in[i, part, :], own_lanes),
-            (lambda part: merged(c_in[2 * i + 1, part, :], c_in[2 * i, part, :]), near),
+            (lambda part: merged(c_full[2 * i + 1, part, :], c_full[2 * i, part, :]), near),
         )
         for source, lanes in pieces:
             relax[rows, lanes] = source(slice(38, 40))
@@ -402,6 +444,9 @@
             pltpu.SMEM((1, 1, 2), i32),
             pltpu.VMEM((2, MESSAGE, SPAN), f32),
             pltpu.VMEM((2, MESSAGE, SPAN), f32),
+            pltpu.VMEM((4, CORNER, LANES), f32),
+            pltpu.VMEM((4, CORNER, LANES), f32),
+            pltpu.VMEM((4, 16, LANES), f32),
             pltpu.VMEM((4, MESSAGE, LANES), f32),
             pltpu.VMEM((2, 19, ROWS, LANES), f32),
             pltpu.VMEM((2, ROWS, LANES), f32),

time: 37.6 us -> 37.1 us (0.987)
  Pallas kernels: 36.8 us -> 36.3 us
    pallas_call x1, Pallas kernels: 35.8 us -> 35.3 us  [local(): pl.pallas_call(kernel, out_shape=(jax.ShapeDtypeStruct((19, ROWS, SPAN),...]
where the time goes in v4:
time: 37.1 us; the launch traced here: 36.9 us
  Pallas kernels  36.3 us (98%)
  between operations  0.64 us (2%)
    pallas_call x1, Pallas kernels, local(): pl.pallas_call(kernel, out_shape=(jax.ShapeDtypeStruct((19, ROWS, SPAN),...  35.3 us
    pallas_call x1, Pallas kernels, local(): pl.pallas_call(store, out_shape=tuple((jax.ShapeDtypeStruct(r.shape, f32)...  0.94 us

profile of v4, /device:TPU:41, one launch (start us, length us, event | category | flops | bytes accessed | tf_op | source)
XLA Modules:
  0.0 36.9 jit_solution(16734048104576496865)
XLA Ops:
  0.6 35.3 %shard_map.59 = (f32[19,16,512]{2,1,0:T(8,128)S(1)}, f32[19,16,256]{2,1,0:T(8,128)S(1)}) custom-call(f32[19,16,512]{2,1,0:T(8,128)} %populations.1, f32[16,512]{1,0:T(8,128)} %relaxation.1, s32[2,16,512]{2,1,0:T(8,128)} %link_flags.1, s32[1,1,2]{2,1,0:T(1,128)} %migrations.1), custom_call_target="tpu_custom_call" | custom-call | flops 8000000 | bytes 2000000 | tf_op jit(solution)/shard_map/pallas_call | solution.py:429
  36.0 0.9 %shard_map.60 = (f32[19,16,512]{2,1,0:T(8,128)}, f32[19,16,256]{2,1,0:T(8,128)}) custom-call(f32[19,16,512]{2,1,0:T(8,128)S(1)} %get-tuple-element.4.final, f32[19,16,256]{2,1,0:T(8,128)S(1)} %get-tuple-element.5.guest), custom_call_target="tpu_custom_call" | custom-call | tf_op jit(solution)/shard_map/pallas_call | solution.py:471
